TPU v7x, 128 devices: a whole 4x4x4 slice. The times are simulated.
128 devices in a mesh: row: 16 (over x_hi, y, core), col: 8 (over z, x_lo).
Axes of the slice: x: 4 (x_hi: 2, x_lo: 2; x = x_hi * 2 + x_lo), y: 4, z: 4, core: 2. Of those that a mesh axis runs over, the one named last changes fastest.
Arguments:
- block_input: bfloat16 [512, 512, 256], P('row', 'col'), may hold values from -6 to 6
- cotangent: bfloat16 [512, 512, 256], P('row', 'col'), may hold values from -6 to 6
- conv_gain: float32 [256], replicated, may hold values from 0.25 to 1.75
- grid_gain: float32 [256], replicated, may hold values from 0.25 to 1.75
- mlp_gain: float32 [256], replicated, may hold values from 0.25 to 1.75
- expand_weight: bfloat16 [256, 1024], replicated, may hold values from -0.375 to 0.375
- depth_kernel: bfloat16 [3, 3, 1024], replicated, may hold values from -2 to 2
- shrink_weight: bfloat16 [1024, 256], replicated, may hold values from -0.1875 to 0.1875
- qkv_weight: bfloat16 [256, 768], replicated, may hold values from -0.375 to 0.375
- mix_weight: bfloat16 [256, 256], replicated, may hold values from -0.375 to 0.375
- grid_bias: float32 [8, 64, 64], replicated, may hold values from -3 to 320
- widen_weight: bfloat16 [256, 1024], replicated, may hold values from -0.375 to 0.375
- narrow_weight: bfloat16 [1024, 256], replicated, may hold values from -0.1875 to 0.1875
Outputs:
- block_out: bfloat16 [512, 512, 256], P('row', 'col')
- input_grad: bfloat16 [512, 512, 256], P('row', 'col')
- qkv_grad: float32 [256, 768], replicated
- mix_grad: float32 [256, 256], replicated
All inputs are finite; a program needn't handle non-finite values.
Results may differ from a plain program's by a relative error of at most 0.017.
Values may be sent and summed in bfloat16 or wider, within the bound.
A program may use at most 192 MiB of HBM per device.

v0:
```python
import math

import jax
import jax.numpy as jnp
from jax import lax
from jax.sharding import PartitionSpec as P

HEADS = 8
GRID = 8


def padded_2(cells, sides, width):
    for axis, dim in sides:
        count = lax.axis_size(axis)
        ends = count - 1
        head = lax.slice_in_dim(cells, 0, width, axis=dim)
        tail = lax.slice_in_dim(cells, cells.shape[dim] - width, cells.shape[dim], axis=dim)
        cells = jnp.concatenate(
            [
                lax.ppermute(tail, axis, [(i, (i + 1) % count) for i in range(ends)]),
                cells,
                lax.ppermute(head, axis, [((i + 1) % count, i) for i in range(ends)]),
            ],
            axis=dim,
        )
    return cells


def rounded(values):
    return lax.optimization_barrier(values.astype(jnp.bfloat16))


def gelu_tanh(inputs):
    inner = 0.7978845608028654 * (inputs + 0.044715 * inputs * inputs * inputs)
    return 0.5 * inputs * (1.0 + jnp.tanh(inner))


def gelu_slope(inputs):
    inner = 0.7978845608028654 * (inputs + 0.044715 * inputs * inputs * inputs)
    tangent = jnp.tanh(inner)
    return 0.5 * (1.0 + tangent) + 0.5 * inputs * (1.0 - tangent * tangent) * 0.7978845608028654 * (
        1.0 + 3.0 * 0.044715 * inputs * inputs
    )


def layer_norm(values, gain):
    widened = values.astype(jnp.float32)
    centre = widened - jnp.mean(widened, axis=-1, keepdims=True)
    inv_std = lax.rsqrt(jnp.mean(centre * centre, axis=-1, keepdims=True) + 1e-05)
    return rounded(centre * inv_std * gain)


def norm_back(cotan, values, gain):
    widened = values.astype(jnp.float32)
    centre = widened - jnp.mean(widened, axis=-1, keepdims=True)
    inv_std = lax.rsqrt(jnp.mean(centre * centre, axis=-1, keepdims=True) + 1e-05)
    normal = centre * inv_std
    scaled = cotan.astype(jnp.float32) * gain
    return inv_std * (
        scaled
        - jnp.mean(scaled, axis=-1, keepdims=True)
        - normal * jnp.mean(scaled * normal, axis=-1, keepdims=True)
    )


def dense_product(left, right):
    return jnp.dot(left, right, preferred_element_type=jnp.float32)


def dense_transposed(left, right):
    return lax.dot_general(
        left, right, (((left.ndim - 1,), (1,)), ((), ())), preferred_element_type=jnp.float32
    )


def outer_sum(left, right):
    flat_left = left.reshape(-1, left.shape[-1])
    flat_right = right.reshape(-1, right.shape[-1])
    return lax.dot_general(
        flat_left, flat_right, (((0,), (0,)), ((), ())), preferred_element_type=jnp.float32
    )


def depthwise(padded, kernel):
    out_rows = padded.shape[0] - 2
    out_cols = padded.shape[1] - 2
    running = jnp.zeros((out_rows, out_cols, padded.shape[2]), jnp.float32)
    for shift_row in range(3):
        for shift_col in range(3):
            window = padded[
                shift_row : shift_row + out_rows, shift_col : shift_col + out_cols
            ].astype(jnp.float32)
            running = running + window * kernel[shift_row, shift_col].astype(jnp.float32)
    return running


def depth_back(padded, kernel):
    out_rows = padded.shape[0] - 2
    out_cols = padded.shape[1] - 2
    running = jnp.zeros((out_rows, out_cols, padded.shape[2]), jnp.float32)
    for shift_row in range(3):
        for shift_col in range(3):
            window = padded[
                2 - shift_row : 2 - shift_row + out_rows, 2 - shift_col : 2 - shift_col + out_cols
            ].astype(jnp.float32)
            running = running + window * kernel[shift_row, shift_col].astype(jnp.float32)
    return running


def attend(normed_sets, qkv_weight, mix_weight, grid_bias):
    set_count, members, channels = normed_sets.shape
    head_dim = channels // HEADS
    qkv_sets = rounded(dense_product(normed_sets, qkv_weight))
    heads_split = qkv_sets.reshape(set_count, members, 3, HEADS, head_dim)
    queries = heads_split[:, :, 0]
    key_heads = heads_split[:, :, 1]
    values = heads_split[:, :, 2]
    scores = (
        jnp.einsum("smhd,snhd->shmn", queries, key_heads, preferred_element_type=jnp.float32)
        / math.sqrt(head_dim)
        + grid_bias[None]
    )
    row_max = jnp.max(scores, axis=-1, keepdims=True)
    exponent = jnp.exp(scores - row_max)
    softmax_weights = exponent / jnp.sum(exponent, axis=-1, keepdims=True)
    low_weights = rounded(softmax_weights)
    mixed = rounded(
        jnp.einsum(
            "shmn,snhd->smhd", low_weights, values, preferred_element_type=jnp.float32
        ).reshape(set_count, members, channels)
    )
    projected = rounded(dense_product(mixed, mix_weight))
    return (qkv_sets, softmax_weights, mixed, projected)


def attend_back(normed_sets, qkv_sets, softmax_weights, mixed, grad_sets, qkv_weight, mix_weight):
    set_count, members, channels = normed_sets.shape
    head_dim = channels // HEADS
    mix_part = outer_sum(mixed, grad_sets)
    mixed_grad = rounded(dense_transposed(grad_sets, mix_weight)).reshape(
        set_count, members, HEADS, head_dim
    )
    heads_split = qkv_sets.reshape(set_count, members, 3, HEADS, head_dim)
    queries = heads_split[:, :, 0]
    key_heads = heads_split[:, :, 1]
    values = heads_split[:, :, 2]
    weight_grad = jnp.einsum(
        "smhd,snhd->shmn", mixed_grad, values, preferred_element_type=jnp.float32
    )
    low_weights = rounded(softmax_weights)
    value_grad = jnp.einsum(
        "shmn,smhd->snhd", low_weights, mixed_grad, preferred_element_type=jnp.float32
    )
    centre = jnp.sum(softmax_weights * weight_grad, axis=-1, keepdims=True)
    score_grad = rounded(softmax_weights * (weight_grad - centre) / math.sqrt(head_dim))
    query_grad = jnp.einsum(
        "shmn,snhd->smhd", score_grad, key_heads, preferred_element_type=jnp.float32
    )
    key_grad = jnp.einsum(
        "shmn,smhd->snhd", score_grad, queries, preferred_element_type=jnp.float32
    )
    qkv_grad_sets = rounded(
        jnp.stack([query_grad, key_grad, value_grad], axis=2).reshape(
            set_count, members, 3 * channels
        )
    )
    qkv_part = outer_sum(normed_sets, qkv_grad_sets)
    normed_grad = rounded(dense_transposed(qkv_grad_sets, qkv_weight))
    return (qkv_part, mix_part, normed_grad)


def mlp_pass(section_two, cotangent, mlp_gain, widen_weight, narrow_weight):
    normed_mlp = layer_norm(section_two, mlp_gain)
    widen_pre = dense_product(normed_mlp, widen_weight)
    widen_act = rounded(gelu_tanh(widen_pre))
    block_out = rounded(section_two.astype(jnp.float32) + dense_product(widen_act, narrow_weight))
    widen_grad = rounded(dense_transposed(cotangent, narrow_weight) * gelu_slope(widen_pre))
    section_two_grad = rounded(
        cotangent.astype(jnp.float32)
        + norm_back(dense_transposed(widen_grad, widen_weight), section_two, mlp_gain)
    )
    return (block_out, section_two_grad)


def sets_outgoing(tile):
    tile_rows, tile_cols, channels = tile.shape
    row_dev = lax.axis_size("row")
    col_dev = lax.axis_size("col")
    row_part = tile_rows // row_dev
    col_part = tile_cols // col_dev
    outgoing = tile.reshape(row_dev, row_part, col_part, col_dev, channels).transpose(0, 3, 1, 2, 4)
    return outgoing.reshape(row_dev * col_dev, row_part, col_part, channels)


def sets_arrange(arrived, tile_rows, tile_cols):
    channels = arrived.shape[-1]
    row_dev = lax.axis_size("row")
    col_dev = lax.axis_size("col")
    row_part = tile_rows // row_dev
    spread = row_dev // GRID
    col_fold = GRID // col_dev
    inner_cols = tile_cols // GRID
    shaped = arrived.reshape(GRID, spread, col_dev, row_part, col_fold, inner_cols, channels)
    ordered = shaped.transpose(1, 3, 5, 0, 2, 4, 6)
    return ordered.reshape(spread * row_part * inner_cols, GRID * GRID, channels)


def tiles_outgoing(sets, tile_rows, tile_cols):
    channels = sets.shape[-1]
    row_dev = lax.axis_size("row")
    col_dev = lax.axis_size("col")
    row_part = tile_rows // row_dev
    col_part = tile_cols // col_dev
    spread = row_dev // GRID
    col_fold = GRID // col_dev
    inner_cols = tile_cols // GRID
    grouped = sets.reshape(spread, row_part, inner_cols, GRID, col_dev, col_fold, channels)
    return grouped.transpose(3, 0, 4, 1, 5, 2, 6).reshape(
        row_dev * col_dev, row_part, col_part, channels
    )


def tiles_arrange(arrived, tile_rows, tile_cols):
    channels = arrived.shape[-1]
    row_dev = lax.axis_size("row")
    col_dev = lax.axis_size("col")
    row_part = tile_rows // row_dev
    col_part = tile_cols // col_dev
    arrived = arrived.reshape(row_dev, col_dev, row_part, col_part, channels).transpose(
        0, 2, 3, 1, 4
    )
    return arrived.reshape(tile_rows, tile_cols, channels)


def gather_sets(tile):
    outgoing = sets_outgoing(tile)
    arrived = lax.all_to_all(outgoing, ("row", "col"), split_axis=0, concat_axis=0, tiled=True)
    return sets_arrange(arrived, tile.shape[0], tile.shape[1])


def return_tiles(sets, tile_rows, tile_cols):
    outgoing = tiles_outgoing(sets, tile_rows, tile_cols)
    arrived = lax.all_to_all(outgoing, ("row", "col"), split_axis=0, concat_axis=0, tiled=True)
    return tiles_arrange(arrived, tile_rows, tile_cols)


def body(
    block_input,
    cotangent,
    conv_gain,
    grid_gain,
    mlp_gain,
    expand_weight,
    depth_kernel,
    shrink_weight,
    qkv_weight,
    mix_weight,
    grid_bias,
    widen_weight,
    narrow_weight,
):
    tile_rows, tile_cols, channels = block_input.shape
    normed_conv = layer_norm(block_input, conv_gain)
    expand_pre = dense_product(normed_conv, expand_weight)
    expand_act = rounded(gelu_tanh(expand_pre))
    act_padded = padded_2(expand_act, (("row", 0), ("col", 1)), 1)
    depth_pre = depthwise(act_padded, depth_kernel)
    depth_act = rounded(gelu_tanh(depth_pre))
    section_one = rounded(block_input.astype(jnp.float32) + dense_product(depth_act, shrink_weight))
    normed_grid = layer_norm(section_one, grid_gain)
    grid_sets = gather_sets(normed_grid)
    qkv_sets, softmax_weights, mixed_sets, projected_sets = attend(
        grid_sets, qkv_weight, mix_weight, grid_bias
    )
    grid_out = return_tiles(projected_sets, tile_rows, tile_cols)
    section_two = rounded(section_one.astype(jnp.float32) + grid_out.astype(jnp.float32))
    block_out, section_two_grad = mlp_pass(
        section_two, cotangent, mlp_gain, widen_weight, narrow_weight
    )
    grad_sets = gather_sets(section_two_grad)
    qkv_part, mix_part, normed_grad_sets = attend_back(
        grid_sets, qkv_sets, softmax_weights, mixed_sets, grad_sets, qkv_weight, mix_weight
    )
    normed_grad = return_tiles(normed_grad_sets, tile_rows, tile_cols)
    section_one_grad = rounded(
        section_two_grad.astype(jnp.float32) + norm_back(normed_grad, section_one, grid_gain)
    )
    depth_grad = rounded(dense_transposed(section_one_grad, shrink_weight) * gelu_slope(depth_pre))
    grad_padded = padded_2(depth_grad, (("row", 0), ("col", 1)), 1)
    hidden_grad = depth_back(grad_padded, depth_kernel)
    expand_grad = rounded(hidden_grad * gelu_slope(expand_pre))
    input_grad = rounded(
        section_one_grad.astype(jnp.float32)
        + norm_back(dense_transposed(expand_grad, expand_weight), block_input, conv_gain)
    )
    qkv_total, mix_total = lax.psum((qkv_part, mix_part), ("row", "col"))
    factor = 1.0 / math.sqrt(tile_rows * tile_cols * lax.axis_size("row") * lax.axis_size("col"))
    return (block_out, input_grad, qkv_total * factor, mix_total * factor)


def solution(mesh):
    placed = (
        P("row", "col", None),
        P("row", "col", None),
        P(),
        P(),
        P(),
        P(),
        P(),
        P(),
        P(),
        P(),
        P(),
        P(),
        P(),
    )
    return jax.shard_map(
        body,
        mesh=mesh,
        in_specs=placed,
        out_specs=(P("row", "col", None), P("row", "col", None), P(), P()),
        check_vma=False,
    )
```

profile of v0, /device:TPU:3, one launch (start us, length us, event | category | flops | bytes accessed | tf_op | source)
XLA Modules:
  0.0 457.6 jit_solution(3818835933065443114)
XLA Ops:
  7.2 1.6 convert_reduce_fusion.2
  8.8 1.9 fusion.64
  11.3 1.8 fusion.58
  13.1 6.0 %multiply_convert_fusion.3 = (bf16[32,64,1024]{2,1,0:T(8,128)(2,1)S(1)}, f32[32,64,1024]{2,1,0:T(8,128)}) fusion(bf16[32,64,256]{2,1,0:T(8,128)(2,1)S(1)} %fusion.58, bf16[256,1024]{1,0:T(8,128)(2,1)} %param.18), kind=kOutput, calls=%fused_computation.37 | convolution fusion | flops 1092616192 | bytes 14155776 | tf_op jit(solution)/shard_map/dot_general | solution.py:67
  19.2 3.8 collective-permute-start
  22.9 1.9 collective-permute-start.1
  24.9 4.3 collective-permute-done.1
  29.5 3.5 collective-permute-start.2
  33.0 1.9 collective-permute-start.3
  35.9 3.7 collective-permute-done.3
  39.7 3.3 maximum_maximum_fusion
  43.0 14.2 %multiply_convert_fusion.2 = (bf16[32,64,1024]{2,1,0:T(8,128)(2,1)S(1)}, f32[32,64,1024]{2,1,0:T(8,128)}) fusion(f32[1024]{0:T(1024)S(1)} %bitcast.199, bf16[34,65,1024]{2,1,0:T(8,128)(2,1)S(1)} %get-tuple-element.17, f32[1024]{0:T(1024)S(1)} %bitcast.201, bf16[1,64,1024]{2,1,0:T(8,128)(2,1)S(1)} %collective-permute-done.1, ...), kind=kLoop, calls=%fused_computation.35 | loop fusion | flops 77594624 | bytes 42242048 | tf_op jit(solution)/shard_map/convert_element_type | solution.py:30
  57.3 1.3 fusion.66
  61.6 13.1 %all-to-all-start = ((bf16[128,2,8,256]{3,2,1,0:T(8,128)(2,1)}), bf16[128,2,8,256]{3,2,1,0:T(8,128)(2,1)S(1)}, u32[]{:S(2)}, u32[]{:S(2)}) async-start(bf16[128,2,8,256]{3,2,1,0:T(8,128)(2,1)} %bitcast.178), calls=%async_computation | async-start | bytes 2097152 | tf_op jit(solution)/shard_map/all_to_all | solution.py:237
  75.8 16.0 %all-to-all-done = bf16[128,2,8,256]{3,2,1,0:T(8,128)(2,1)S(1)} async-done(((bf16[128,2,8,256]{3,2,1,0:T(8,128)(2,1)}), bf16[128,2,8,256]{3,2,1,0:T(8,128)(2,1)S(1)}, u32[]{:S(2)}, u32[]{:S(2)}) %all-to-all-start) | async-done | bytes 1048608 | tf_op jit(solution)/shard_map/all_to_all | solution.py:237
  93.1 2.6 convolution_convert_fusion
  95.7 6.6 %copy.77 = bf16[32,64,768]{1,2,0:T(8,128)(2,1)} copy(bf16[32,64,768]{2,1,0:T(8,128)(2,1)} %convolution_convert_fusion) | data formatting | bytes 6291456 | tf_op jit(solution)/shard_map/optimization_barrier | solution.py:30
  102.3 6.8 %fusion.70 = f32[32,8,64,64]{2,3,1,0:T(8,128)} fusion(bf16[32,64,3,8,32]{1,4,3,2,0:T(8,128)(2,1)} %bitcast.150), kind=kOutput, calls=%fused_computation.112 | convolution fusion | flops 67108864 | bytes 8388608 | tf_op jit(solution)/shard_map/smhd,snhd->shmn/dot_general | solution.py:119
  109.2 8.9 %fusion.91 = (f32[32,8,64]{2,1,0:T(8,128)S(1)}, f32[32,8,64,64]{2,3,1,0:T(8,128)S(1)}) fusion(f32[32,8,64,64]{2,3,1,0:T(8,128)} %fusion.70, f32[8,64,64]{1,2,0:T(8,128)S(1)} %copy.81), kind=kOutput, calls=%fused_computation.167 | output fusion | flops 6291519 | bytes 8585216 | tf_op jit(solution)/shard_map/sub | solution.py:124
  118.1 1.5 fusion.88
  119.6 1.7 copy-done.8
  121.4 4.4 convolution_convert_fusion.1
  127.1 23.8 %all_to_all.20 = bf16[128,2,8,256]{3,2,1,0:T(8,128)(2,1)S(1)} all-to-all(bf16[128,2,8,256]{3,2,1,0:T(8,128)(2,1)S(1)} %bitcast.179), channel_id=1, replica_groups=mesh['row'=16,'col'=8] {'row','col'}, dimensions={0} | all-to-all | bytes 2097152 | tf_op jit(solution)/shard_map/all_to_all | solution.py:243
  151.2 1.6 copy.85
  155.0 4.4 multiply_convert_fusion.1
  159.4 5.9 %fusion.12 = bf16[32,64,1024]{2,1,0:T(8,128)(2,1)S(1)} fusion(f32[32,64,1024]{2,1,0:T(8,128)S(1)} %get-tuple-element.38, bf16[32,64,256]{2,1,0:T(8,128)(2,1)S(1)} %copy-done.24, bf16[1024,256]{1,0:T(8,128)(2,1)S(1)} %copy-done.35), kind=kOutput, calls=%fused_computation.18 | convolution fusion | flops 1113587712 | bytes 14155776 | tf_op jit(solution)/shard_map/dot_general | solution.py:71
  165.3 1.6 multiply_reduce_fusion.2
  167.0 1.3 fusion.49
  170.5 7.8 %all-to-all-start.2 = ((bf16[128,2,8,256]{3,2,1,0:T(8,128)(2,1)}), bf16[128,2,8,256]{3,2,1,0:T(8,128)(2,1)}, u32[]{:S(2)}, u32[]{:S(2)}) async-start(bf16[128,2,8,256]{3,2,1,0:T(8,128)(2,1)} %bitcast.177), calls=%async_computation.2 | async-start | bytes 2097152 | tf_op jit(solution)/shard_map/all_to_all | solution.py:237
  178.3 1.6 copy.99
  180.0 15.1 %all-to-all-done.2 = bf16[128,2,8,256]{3,2,1,0:T(8,128)(2,1)} async-done(((bf16[128,2,8,256]{3,2,1,0:T(8,128)(2,1)}), bf16[128,2,8,256]{3,2,1,0:T(8,128)(2,1)}, u32[]{:S(2)}, u32[]{:S(2)}) %all-to-all-start.2) | async-done | bytes 1048608 | tf_op jit(solution)/shard_map/all_to_all | solution.py:237
  195.1 1.6 copy.87
  197.6 1.4 convolution_convert_fusion.3
  199.1 2.9 copy.88
  202.0 6.6 %convert_bitcast_fusion.2 = bf16[32,64,1,8,32]{1,4,3,0,2:T(8,128)(2,1)} fusion(bf16[32,64,8,32]{1,3,2,0:T(8,128)(2,1)} %bitcast.161, bf16[32,8,64,64]{2,3,1,0:T(8,128)(2,1)} %copy-done.5), kind=kOutput, calls=%fused_computation.107 | convolution fusion | flops 67633152 | bytes 4194304 | tf_op jit(solution)/shard_map/shmn,smhd->snhd/dot_general | solution.py:151
  208.6 4.6 fusion.69
  213.2 13.1 %multiply_convert_fusion = bf16[32,8,64,64]{2,3,1,0:T(8,128)(2,1)S(1)} fusion(f32[32,8,64,64]{2,3,1,0:T(8,128)} %fusion.69, f32[32,8,64,64]{2,3,1,0:T(8,128)} %copy-done.8, f32[32,8,64]{2,1,0:T(8,128)S(1)} %get-tuple-element.35), kind=kOutput, calls=%fused_computation.29 | output fusion | flops 7356479 | bytes 10551296 | tf_op jit(solution)/shard_map/sub | solution.py:155
  226.3 2.3 convert_bitcast_fusion.3
  230.1 1.8 pad_maximum_fusion
  231.9 2.1 copy.92
  234.0 2.6 copy-done.2
  236.7 1.9 convolution_convert_fusion.2
  238.5 1.6 copy.94
  240.1 6.6 %all-to-all-start.3 = ((bf16[128,2,8,256]{3,2,1,0:T(8,128)(2,1)}), bf16[128,2,8,256]{3,2,1,0:T(8,128)(2,1)S(1)}, u32[]{:S(2)}, u32[]{:S(2)}) async-start(bf16[128,2,8,256]{3,2,1,0:T(8,128)(2,1)} %bitcast.175), calls=%async_computation.3 | async-start | bytes 2097152 | tf_op jit(solution)/shard_map/all_to_all | solution.py:243
  246.8 4.4 fusion.68
  251.2 7.0 %copy.98 = bf16[32,64,768]{2,1,0:T(8,128)(2,1)} copy(bf16[32,64,768]{1,2,0:T(8,128)(2,1)} %bitcast.149) | data formatting | bytes 6291456 | tf_op jit(solution)/shard_map/optimization_barrier | solution.py:30
  258.1 2.4 fusion.93
  260.5 4.1 fusion.92
  265.7 1.7 copy.95
  268.5 2.4 fusion.56
  271.0 5.9 %fusion.17 = bf16[32,64,1024]{2,1,0:T(8,128)(2,1)S(1)} fusion(f32[32,64,1024]{2,1,0:T(8,128)S(1)} %bitcast.171, bf16[32,64,256]{2,1,0:T(8,128)(2,1)S(1)} %fusion.56, bf16[1024,256]{1,0:T(8,128)(2,1)S(1)} %copy-done.38), kind=kOutput, calls=%fused_computation.23 | convolution fusion | flops 1113587712 | bytes 14155776 | tf_op jit(solution)/shard_map/dot_general | solution.py:71
  276.9 2.0 copy-done.3
  278.9 3.3 collective-permute-start.4
  282.3 1.9 collective-permute-start.5
  284.2 128.8 %all-reduce.3.cloned.1.call-done = (f32[256,768]{1,0:T(8,128)}, f32[256,256]{1,0:T(8,128)}) async-done(((f32[256,768]{1,0:T(8,128)}, f32[256,256]{1,0:T(8,128)}), (f32[256,768]{1,0:T(8,128)}, f32[256,256]{1,0:T(8,128)})) %all-reduce.3.cloned.1.call-update) | async-done | bytes 1048592 | tf_op jit(solution)/shard_map/psum | solution.py:296
  413.0 2.2 broadcast_multiply_fusion
  415.2 1.4 pad_maximum_fusion.9
  416.7 3.0 collective-permute-start.6
  419.7 3.4 collective-permute-start.7
  423.8 2.8 collective-permute-done.7
  426.6 3.2 pad_maximum_fusion.2
  429.9 15.8 %fusion.22 = bf16[32,64,1024]{2,1,0:T(8,128)(2,1)S(1)} fusion(f32[32,64,1024]{2,1,0:T(8,128)S(1)} %bitcast.169, bf16[32,64,1024]{2,1,0:T(8,128)(2,1)S(1)} %copy-done.4, bf16[34,65,1024]{2,1,0:T(8,128)(2,1)S(1)} %get-tuple-element.13, bf16[1,64,1024]{2,1,0:T(8,128)(2,1)S(1)} %collective-permute-done.4, bf16[34,65,1024]{2,1,0:T(8,128)(2,1)S(1)} %get-tuple-element.12, ...), kind=kLoop, calls=%fused_computation.28 | loop fusion | flops 98566144 | bytes 42242048 | tf_op jit(solution)/shard_map/convert_element_type | solution.py:30
  445.7 2.7 multiply_reduce_fusion.1
  448.5 2.1 fusion.63
  (134 shorter events, 18.8 us)
Async XLA Ops:
  7.2 147.8 %copy-start = (bf16[256,1024]{1,0:T(8,128)(2,1)S(1)}, bf16[256,1024]{1,0:T(8,128)(2,1)}, u32[]{:S(2)}) copy-start(bf16[256,1024]{1,0:T(8,128)(2,1)} %param.24) | copy-start | bytes 1572868
  8.8 1.9 copy-start.26
  10.7 0.6 copy-start.29
  13.1 21.8 %copy-start.31 = (bf16[3,3,1024]{2,1,0:T(4,128)(2,1)S(1)}, bf16[3,3,1024]{2,1,0:T(4,128)(2,1)}, u32[]{:S(2)}) copy-start(bf16[3,3,1024]{2,1,0:T(4,128)(2,1)} %param.19) | copy-start | bytes 55300
  19.2 5.7 %collective-permute-start = (bf16[1,64,1024]{2,1,0:T(8,128)(2,1)S(1)}, bf16[1,64,1024]{2,1,0:T(8,128)(2,1)S(1)}, u32[]{:S(2)}, u32[]{:S(2)}) collective-permute-start(bf16[1,64,1024]{2,1,0:T(8,128)(2,1)S(1)} %get-tuple-element.22), channel_id=1, source_target_pairs={{0,8},{8,16},{16,24},{24,32},{32,40},{40,48},{48,56},{56,64},{64,7... | collective-permute-start | bytes 393224 | tf_op jit(solution)/shard_map/ppermute | solution.py:20
  22.9 6.3 %collective-permute-start.1 = (bf16[1,64,1024]{2,1,0:T(8,128)(2,1)S(1)}, bf16[1,64,1024]{2,1,0:T(8,128)(2,1)S(1)}, u32[]{:S(2)}, u32[]{:S(2)}) collective-permute-start(bf16[1,64,1024]{2,1,0:T(8,128)(2,1)S(1)} %get-tuple-element.23), channel_id=1, source_target_pairs={{8,0},{16,8},{24,16},{32,24},{40,32},{48,40},{56,48},{64,56},{72,6... | collective-permute-start | bytes 393224 | tf_op jit(solution)/shard_map/ppermute | solution.py:22
  29.5 6.5 %collective-permute-start.2 = (bf16[34,1,1024]{2,1,0:T(2,128)(2,1)S(1)}, bf16[34,1,1024]{2,1,0:T(2,128)(2,1)S(1)}, u32[]{:S(2)}, u32[]{:S(2)}) collective-permute-start(bf16[34,1,1024]{2,1,0:T(2,128)(2,1)S(1)} %get-tuple-element.18), channel_id=1, source_target_pairs={{0,1},{1,2},{2,3},{3,4},{4,5},{5,6},{6,7},{8,9},{9,10},{10,11},{11... | collective-permute-start | bytes 208904 | tf_op jit(solution)/shard_map/ppermute | solution.py:20
  33.0 6.7 %collective-permute-start.3 = (bf16[34,1,1024]{2,1,0:T(2,128)(2,1)S(1)}, bf16[34,1,1024]{2,1,0:T(2,128)(2,1)S(1)}, u32[]{:S(2)}, u32[]{:S(2)}) collective-permute-start(bf16[34,1,1024]{2,1,0:T(2,128)(2,1)S(1)} %get-tuple-element.19), channel_id=1, source_target_pairs={{1,0},{2,1},{3,2},{4,3},{5,4},{6,5},{7,6},{9,8},{10,9},{11,10},{12... | collective-permute-start | bytes 208904 | tf_op jit(solution)/shard_map/ppermute | solution.py:22
  43.0 14.3 %copy-start.14 = (bf16[32,64,256]{2,1,0:T(8,128)(2,1)S(1)}, bf16[32,64,256]{2,1,0:T(8,128)(2,1)}, u32[]{:S(2)}) copy-start(bf16[32,64,256]{2,1,0:T(8,128)(2,1)} %param.13) | copy-start | bytes 3145732
  43.0 14.3 %copy-start.37 = (bf16[1024,256]{1,0:T(8,128)(2,1)S(1)}, bf16[1024,256]{1,0:T(8,128)(2,1)}, u32[]{:S(2)}) copy-start(bf16[1024,256]{1,0:T(8,128)(2,1)} %param.20) | copy-start | bytes 1572868
  57.3 2.3 copy-start.32
  58.5 94.3 %copy-start.6 = (bf16[32,64,256]{2,1,0:T(8,128)(2,1)}, bf16[32,64,256]{2,1,0:T(8,128)(2,1)S(1)}, u32[]{:S(2)}) copy-start(bf16[32,64,256]{2,1,0:T(8,128)(2,1)S(1)} %fusion.66) | copy-start | bytes 3145732
  58.6 34.5 %copy-start.23 = (bf16[256,768]{1,0:T(8,128)(2,1)S(1)}, bf16[256,768]{1,0:T(8,128)(2,1)}, u32[]{:S(2)}) copy-start(bf16[256,768]{1,0:T(8,128)(2,1)} %param.21) | copy-start | bytes 1179652
  61.6 30.2 %all-to-all-start = ((bf16[128,2,8,256]{3,2,1,0:T(8,128)(2,1)}), bf16[128,2,8,256]{3,2,1,0:T(8,128)(2,1)S(1)}, u32[]{:S(2)}, u32[]{:S(2)}) async-start(bf16[128,2,8,256]{3,2,1,0:T(8,128)(2,1)} %bitcast.178), calls=%async_computation | async-start | bytes 2097152 | tf_op jit(solution)/shard_map/all_to_all | solution.py:237
  92.1 1.0 copy-start.20
  118.1 3.3 copy-start.8
  121.3 5.7 %copy-start.5 = (bf16[32,8,64,64]{2,3,1,0:T(8,128)(2,1)}, bf16[32,8,64,64]{2,3,1,0:T(8,128)(2,1)S(1)}, u32[]{:S(2)}) copy-start(bf16[32,8,64,64]{2,3,1,0:T(8,128)(2,1)S(1)} %fusion.88) | copy-start | bytes 6291460
  121.4 4.4 copy-start.25
  125.7 27.1 %copy-start.11 = (bf16[32,8,32,64]{3,2,1,0:T(8,128)(2,1)}, bf16[32,8,32,64]{3,2,1,0:T(8,128)(2,1)S(1)}, u32[]{:S(2)}) copy-start(bf16[32,8,32,64]{3,2,1,0:T(8,128)(2,1)S(1)} %convolution_convert_fusion.1) | copy-start | bytes 3145732
  150.9 3.4 copy-start.33
  153.2 13.7 %copy-start.9 = (bf16[32,64,256]{2,1,0:T(8,128)(2,1)}, bf16[32,64,256]{2,1,0:T(8,128)(2,1)S(1)}, u32[]{:S(2)}) copy-start(bf16[32,64,256]{2,1,0:T(8,128)(2,1)S(1)} %fusion.67) | copy-start | bytes 3145732
  155.0 4.4 copy-start.24
  155.0 4.4 copy-start.35
  166.9 11.4 %copy-start.12 = (bf16[32,8,32,64]{3,2,1,0:T(8,128)(2,1)S(1)}, bf16[32,8,32,64]{3,2,1,0:T(8,128)(2,1)}, u32[]{:S(2)}) copy-start(bf16[32,8,32,64]{3,2,1,0:T(8,128)(2,1)} %copy-done.11) | copy-start | bytes 3145732
  168.3 1.0 copy-start.18
  170.5 24.6 %all-to-all-start.2 = ((bf16[128,2,8,256]{3,2,1,0:T(8,128)(2,1)}), bf16[128,2,8,256]{3,2,1,0:T(8,128)(2,1)}, u32[]{:S(2)}, u32[]{:S(2)}) async-start(bf16[128,2,8,256]{3,2,1,0:T(8,128)(2,1)} %bitcast.177), calls=%async_computation.2 | async-start | bytes 2097152 | tf_op jit(solution)/shard_map/all_to_all | solution.py:237
  196.7 1.0 copy-start.16
  199.1 9.5 %slice-start = ((s8[6291456]{0:T(1024)(128)(4,1)}), s8[2097152]{0:T(1024)(128)(4,1)S(1)}, s32[]{:S(2)}) async-start(s8[6291456]{0:T(1024)(128)(4,1)} %bitcast.152), calls=%async_computation.5 | async-start | bytes 4194304
  202.0 6.6 %copy-start.13 = (bf16[32,64,256]{1,2,0:T(8,128)(2,1)S(1)}, bf16[32,64,256]{1,2,0:T(8,128)(2,1)}, u32[]{:S(2)}) copy-start(bf16[32,64,256]{1,2,0:T(8,128)(2,1)} %copy.88) | copy-start | bytes 3145732
  202.0 6.6 %slice-start.1 = ((s8[6291456]{0:T(1024)(128)(4,1)}), s8[4194304]{0:T(1024)(128)(4,1)S(1)}, s32[]{:S(2)}) async-start(s8[6291456]{0:T(1024)(128)(4,1)} %bitcast.152), calls=%async_computation.6 | async-start | bytes 8388608
  228.5 1.6 copy-start.19
  234.0 2.7 copy-start.2
  234.0 12.7 %copy-start.10 = (bf16[32,64,256]{2,1,0:T(8,128)(2,1)S(1)}, bf16[32,64,256]{2,1,0:T(8,128)(2,1)}, u32[]{:S(2)}) copy-start(bf16[32,64,256]{2,1,0:T(8,128)(2,1)} %copy-done.9) | copy-start | bytes 3145732
  234.0 12.7 %copy-start.36 = (bf16[1024,256]{1,0:T(8,128)(2,1)S(1)}, bf16[1024,256]{1,0:T(8,128)(2,1)}, u32[]{:S(2)}) copy-start(bf16[1024,256]{1,0:T(8,128)(2,1)} %param.25) | copy-start | bytes 1572868
  240.1 24.6 %all-to-all-start.3 = ((bf16[128,2,8,256]{3,2,1,0:T(8,128)(2,1)}), bf16[128,2,8,256]{3,2,1,0:T(8,128)(2,1)S(1)}, u32[]{:S(2)}, u32[]{:S(2)}) async-start(bf16[128,2,8,256]{3,2,1,0:T(8,128)(2,1)} %bitcast.175), calls=%async_computation.3 | async-start | bytes 2097152 | tf_op jit(solution)/shard_map/all_to_all | solution.py:243
  246.7 166.3 %all-reduce.3.cloned.1.call-start = ((), (), s32[]{:S(2)}) async-start(), calls=%async_computation.4 | async-start | bytes 2097152 | tf_op jit(solution)/shard_map/psum | solution.py:296
  251.2 7.0 %copy-start.17 = (bf16[2,2,8,8,8,1,256]{6,4,3,2,1,0,5:T(8,128)(2,1)S(1)}, bf16[2,2,8,8,8,1,256]{6,4,3,2,1,0,5:T(8,128)(2,1)}, u32[]{:S(2)}) copy-start(bf16[2,2,8,8,8,1,256]{6,4,3,2,1,0,5:T(8,128)(2,1)} %copy-done.16) | copy-start | bytes 3145732
  264.6 2.8 copy-start.7
  265.4 5.5 %slice-start.4 = ((s8[8388608]{0:T(1024)(128)(4,1)}), s8[4194304]{0:T(1024)(128)(4,1)S(1)}, s32[]{:S(2)}) async-start(s8[8388608]{0:T(1024)(128)(4,1)} %bitcast.170), calls=%async_computation.9 | async-start | bytes 8388608
  265.7 5.3 %copy-start.38 = (bf16[1024,256]{1,0:T(8,128)(2,1)S(1)}, bf16[1024,256]{1,0:T(8,128)(2,1)}, u32[]{:S(2)}) copy-start(bf16[1024,256]{1,0:T(8,128)(2,1)} %param.20) | copy-start | bytes 1572868
  267.4 3.6 slice-start.5
  270.9 6.0 %copy-start.21 = (bf16[32,64,256]{2,1,0:T(8,128)(2,1)}, bf16[32,64,256]{2,1,0:T(8,128)(2,1)S(1)}, u32[]{:S(2)}) copy-start(bf16[32,64,256]{2,1,0:T(8,128)(2,1)S(1)} %fusion.56) | copy-start | bytes 3145732
  276.9 2.0 copy-start.3
  278.9 136.3 %collective-permute-start.4 = (bf16[1,64,1024]{2,1,0:T(8,128)(2,1)S(1)}, bf16[1,64,1024]{2,1,0:T(8,128)(2,1)S(1)}, u32[]{:S(2)}, u32[]{:S(2)}) collective-permute-start(bf16[1,64,1024]{2,1,0:T(8,128)(2,1)S(1)} %get-tuple-element.20), channel_id=1, source_target_pairs={{0,8},{8,16},{16,24},{24,32},{32,40},{40,48},{48,56},{56,64},{64,7... | collective-permute-start | bytes 393224 | tf_op jit(solution)/shard_map/ppermute | solution.py:20
  282.3 133.0 %collective-permute-start.5 = (bf16[1,64,1024]{2,1,0:T(8,128)(2,1)S(1)}, bf16[1,64,1024]{2,1,0:T(8,128)(2,1)S(1)}, u32[]{:S(2)}, u32[]{:S(2)}) collective-permute-start(bf16[1,64,1024]{2,1,0:T(8,128)(2,1)S(1)} %get-tuple-element.21), channel_id=1, source_target_pairs={{8,0},{16,8},{24,16},{32,24},{40,32},{48,40},{56,48},{64,56},{72,6... | collective-permute-start | bytes 393224 | tf_op jit(solution)/shard_map/ppermute | solution.py:22
  413.0 10.1 %copy-start.28 = (f32[256,256]{1,0:T(8,128)S(1)}, f32[256,256]{1,0:T(8,128)}, u32[]{:S(2)}) copy-start(f32[256,256]{1,0:T(8,128)} %get-tuple-element.9) | copy-start | bytes 786436
  413.0 13.6 %copy-start.4 = (bf16[32,64,1024]{2,1,0:T(8,128)(2,1)S(1)}, bf16[32,64,1024]{2,1,0:T(8,128)(2,1)}, u32[]{:S(2)}) copy-start(bf16[32,64,1024]{2,1,0:T(8,128)(2,1)} %copy-done.3) | copy-start | bytes 12582916
  416.7 7.2 %collective-permute-start.6 = (bf16[34,1,1024]{2,1,0:T(2,128)(2,1)S(1)}, bf16[34,1,1024]{2,1,0:T(2,128)(2,1)S(1)}, u32[]{:S(2)}, u32[]{:S(2)}) collective-permute-start(bf16[34,1,1024]{2,1,0:T(2,128)(2,1)S(1)} %get-tuple-element.14), channel_id=1, source_target_pairs={{1,0},{2,1},{3,2},{4,3},{5,4},{6,5},{7,6},{9,8},{10,9},{11,10},{12... | collective-permute-start | bytes 208904 | tf_op jit(solution)/shard_map/ppermute | solution.py:22
  419.7 6.9 %collective-permute-start.7 = (bf16[34,1,1024]{2,1,0:T(2,128)(2,1)S(1)}, bf16[34,1,1024]{2,1,0:T(2,128)(2,1)S(1)}, u32[]{:S(2)}, u32[]{:S(2)}) collective-permute-start(bf16[34,1,1024]{2,1,0:T(2,128)(2,1)S(1)} %get-tuple-element.15), channel_id=1, source_target_pairs={{0,1},{1,2},{2,3},{3,4},{4,5},{5,6},{6,7},{8,9},{9,10},{10,11},{11... | collective-permute-start | bytes 208904 | tf_op jit(solution)/shard_map/ppermute | solution.py:20
  423.1 6.7 %slice-start.2 = ((s8[8388608]{0:T(1024)(128)(4,1)}), s8[4194304]{0:T(1024)(128)(4,1)S(1)}, s32[]{:S(2)}) async-start(s8[8388608]{0:T(1024)(128)(4,1)} %bitcast.168), calls=%async_computation.7 | async-start | bytes 8388608
  423.8 6.0 %slice-start.3 = ((s8[8388608]{0:T(1024)(128)(4,1)}), s8[4194304]{0:T(1024)(128)(4,1)S(1)}, s32[]{:S(2)}) async-start(s8[8388608]{0:T(1024)(128)(4,1)} %bitcast.168), calls=%async_computation.8 | async-start | bytes 8388608
  429.8 15.8 %copy-start.15 = (bf16[32,64,256]{2,1,0:T(8,128)(2,1)S(1)}, bf16[32,64,256]{2,1,0:T(8,128)(2,1)}, u32[]{:S(2)}) copy-start(bf16[32,64,256]{2,1,0:T(8,128)(2,1)} %param.13) | copy-start | bytes 3145732
  429.9 15.8 %copy-start.27 = (f32[32,64]{1,0:T(8,128)S(1)}, f32[32,64]{1,0:T(8,128)}, u32[]{:S(2)}) copy-start(f32[32,64]{1,0:T(8,128)} %copy-done.26) | copy-start | bytes 24580
  429.9 15.8 %copy-start.30 = (f32[32,64]{1,0:T(8,128)S(1)}, f32[32,64]{1,0:T(8,128)}, u32[]{:S(2)}) copy-start(f32[32,64]{1,0:T(8,128)} %copy-done.29) | copy-start | bytes 24580
  429.9 15.8 %copy-start.34 = (f32[256]{0:T(256)S(1)}, f32[256]{0:T(256)}, u32[]{:S(2)}) copy-start(f32[256]{0:T(256)} %param.15) | copy-start | bytes 3076
  429.9 20.6 %copy-start.1 = (bf16[256,1024]{1,0:T(8,128)(2,1)S(1)}, bf16[256,1024]{1,0:T(8,128)(2,1)}, u32[]{:S(2)}) copy-start(bf16[256,1024]{1,0:T(8,128)(2,1)} %param.24) | copy-start | bytes 1572868
  445.7 2.7 copy-start.22
Sparse Core Ops, SparseCore 0:
  264.8 148.1 all-reduce.2
where the time goes:
time: 467 us; the launch traced here: 458 us
  waiting for transfers between devices  172 us (37%)
  other arithmetic  83.5 us (18%)
  matrix products  71.2 us (15%)
  starting transfers between devices  50.3 us (11%)
  local copies, waits for them, and re-layouts  41.8 us (9%)
  blocking collectives  23.8 us (5%)
  between operations  15.2 us (3%)
    psum x1, waiting for transfers between devices, body(): qkv_total, mix_total = lax.psum((qkv_part, mix_part), ('row', 'col'))  129 us
    convert_element_type x10, other arithmetic, rounded(): return lax.optimization_barrier(values.astype(jnp.bfloat16))  40.9 us
    all_to_all x2, waiting for transfers between devices, gather_sets(): lax.all_to_all(outgoing, ('row', 'col'), split_axis=0, concat_axis=0, til...  31.1 us
    all_to_all x1, blocking collectives, return_tiles(): lax.all_to_all(outgoing, ('row', 'col'), split_axis=0, concat_axis=0, til...  23.8 us
    all_to_all x2, starting transfers between devices, gather_sets(): lax.all_to_all(outgoing, ('row', 'col'), split_axis=0, concat_axis=0, til...  20.9 us
    dot_general x6, matrix products, dense_product(): return jnp.dot(left, right, preferred_element_type=jnp.float32)  19.5 us
    dot_general x6, matrix products, dense_transposed(): lax.dot_general(left, right, (((left.ndim - 1,), (1,)), ((), ())), prefer...  19.4 us
    optimization_barrier x4, local copies, waits for them, and re-layouts, rounded(): return lax.optimization_barrier(values.astype(jnp.bfloat16))  18.1 us
  transfers between devices with their start and end apart: 12, of which 7 were waited for; matrix products, arithmetic and copies ran while one was open for 8% of the time, Pallas kernels for 0%

commit v1 on v0

v1 whole, which is shorter than its diff:
```python
import functools
import math

import jax
import jax.numpy as jnp
from jax import lax
from jax.experimental import pallas as pl
from jax.experimental.pallas import tpu as pltpu
from jax.sharding import PartitionSpec as P

F32 = jnp.float32
BF16 = jnp.bfloat16
MESH = pl.DeviceIdType.MESH
HEADS = 8
EPS = 1e-05
C0 = 0.7978845608028654
C1 = 0.7978845608028654 * 0.044715
MIB = 1024 * 1024


def mm(left, right):
    return jnp.dot(left, right, preferred_element_type=F32)


def mm_nt(left, right):
    return lax.dot_general(left, right, (((1,), (1,)), ((), ())), preferred_element_type=F32)


def mm_tn(left, right):
    return lax.dot_general(left, right, (((0,), (0,)), ((), ())), preferred_element_type=F32)


def stats(values):
    wide = values.astype(F32)
    centre = wide - jnp.mean(wide, axis=-1, keepdims=True)
    inv = lax.rsqrt(jnp.mean(centre * centre, axis=-1, keepdims=True) + EPS)
    return centre * inv, inv


def norm(values, gain):
    normal, _ = stats(values)
    return (normal * gain).astype(BF16)


def norm_back(cotan, values, gain):
    normal, inv = stats(values)
    scaled = cotan * gain
    return inv * (
        scaled
        - jnp.mean(scaled, axis=-1, keepdims=True)
        - normal * jnp.mean(scaled * normal, axis=-1, keepdims=True)
    )


def gelu_both(u):
    w = C1 * (u * u)
    t = jnp.tanh(u * (w + C0))
    p = 0.5 * t + 0.5
    h = u * p
    slope = p + (h * (1.0 - p)) * (6.0 * w + 2.0 * C0)
    return h, slope


def kernel(
    x_ref, cot_ref, cg_ref, gg_ref, mg_ref, we_ref, kf_ref, ws_ref, wqkv_ref, wmix_ref, bias_ref,
    ww_ref, wn_ref, perm_ref,
    out_ref, grad_ref, qg_ref, mxg_ref,
    h_ref, s1_ref, s2_ref, blk_ref, side_ref, halo_ref, hh_ref, xcol_ref, colf_ref, edge_ref,
    x1_ref, n2h_ref, rb_ref, n2s_ref, qs_ref, ks_ref, vs_ref, ps_ref, mxs_ref, mx_ref, mh_ref,
    x2_ref, h3_ref, dx2_ref, dm_ref, rb2_ref, dns_ref, dq_ref, dk_ref, dv_ref, dn_ref, dnh_ref, dx1_ref,
    drow_ref, dcol_ref, dcorn_ref, ccol_ref, g_ref, gb_ref, r1_ref, t1_ref, r2_ref, a3_ref, a4_ref,
    ssem, rsem, hs_sem, hr_sem, ds_sem, dr_sem, as_sem, ar_sem,
):
    row = lax.axis_index("row")
    col = lax.axis_index("col")
    core = lax.rem(row, 2)
    gi = lax.div(row, 2)
    me = gi * 8 + col
    px = lax.div(gi, 4) * 2 + lax.rem(col, 2)
    py = lax.rem(gi, 4)
    pz = lax.div(col, 2)
    nrow, ncol = 16, 8

    halo_ref[...] = jnp.zeros(halo_ref.shape, BF16)
    xcol_ref[...] = jnp.zeros(xcol_ref.shape, BF16)
    drow_ref[...] = jnp.zeros(drow_ref.shape, BF16)
    dcol_ref[...] = jnp.zeros(dcol_ref.shape, BF16)
    dcorn_ref[...] = jnp.zeros(dcorn_ref.shape, BF16)

    barrier = pltpu.get_barrier_semaphore()

    def greet(t, carry):
        r = lax.rem(row + lax.div(t, ncol), nrow)
        c = lax.rem(col + lax.rem(t, ncol), ncol)
        pl.semaphore_signal(barrier, inc=1, device_id=(r, c), device_id_type=MESH)
        return carry

    lax.fori_loop(1, nrow * ncol, greet, 0)

    for i in range(32):
        colf_ref[0, i : i + 1, 0:256] = x_ref[4 * i].astype(F32)[0:1]
        colf_ref[1, i : i + 1, 0:256] = x_ref[4 * i + 3].astype(F32)[15:16]
    xcol_ref[0] = colf_ref[0, :, 0:256].astype(BF16)
    xcol_ref[1] = colf_ref[1, :, 0:256].astype(BF16)

    cg = cg_ref[...]
    gg = gg_ref[...]
    mg = mg_ref[...]

    def expand_block(b, carry):
        n1 = norm(x_ref[pl.ds(16 * b, 16)].reshape(256, 256), cg)
        for l in range(4):
            lanes = slice(256 * l, 256 * l + 256)
            h, slope = gelu_both(mm(n1, we_ref[:, lanes]))
            h_ref[pl.ds(1 + 4 * b, 4), :, lanes] = h.astype(BF16).reshape(4, 64, 256)
            s1_ref[pl.ds(4 * b, 4), :, lanes] = slope.astype(BF16).reshape(4, 64, 256)
        return carry

    lax.fori_loop(0, 4, expand_block, 0)
    pl.semaphore_wait(barrier, nrow * ncol - 1)

    def neighbours(edge, send, source, target, s_sem, r_sem):
        for idx, dr, dc in edge:
            there_r, there_c = row + dr, col + dc
            ok = (there_r >= 0) & (there_r < nrow) & (there_c >= 0) & (there_c < ncol)
            back_r, back_c = row - dr, col - dc
            ok_back = (back_r >= 0) & (back_r < nrow) & (back_c >= 0) & (back_c < ncol)
            copy = pltpu.make_async_remote_copy(
                src_ref=source(idx), dst_ref=target(idx), send_sem=s_sem.at[idx],
                recv_sem=r_sem.at[idx], device_id=(there_r, there_c), device_id_type=MESH,
            )
            if send == 0:
                pl.when(ok)(copy.start)
            elif send == 1:
                pl.when(ok_back)(copy.wait_recv)
            else:
                pl.when(ok)(copy.wait_send)

    edges = (
        (0, -1, 0), (1, 1, 0), (2, 0, -1), (3, 0, 1),
        (4, -1, -1), (5, -1, 1), (6, 1, -1), (7, 1, 1),
    )

    def x_source(idx):
        return (
            x_ref.at[pl.ds(0, 4)], x_ref.at[pl.ds(124, 4)], xcol_ref.at[0], xcol_ref.at[1],
            x_ref.at[0], x_ref.at[3], x_ref.at[124], x_ref.at[127],
        )[idx]

    def x_target(idx):
        return (
            halo_ref.at[pl.ds(4, 4)], halo_ref.at[pl.ds(0, 4)], xcol_ref.at[3], xcol_ref.at[2],
            halo_ref.at[15], halo_ref.at[14], halo_ref.at[13], halo_ref.at[12],
        )[idx]

    neighbours(edges, 0, x_source, x_target, hs_sem, hr_sem)
    lax.fori_loop(4, 8, expand_block, 0)
    neighbours(edges, 1, x_source, x_target, hs_sem, hr_sem)

    halo_ref[8:10] = xcol_ref[2].reshape(2, 16, 256)
    halo_ref[10:12] = xcol_ref[3].reshape(2, 16, 256)
    n1 = norm(halo_ref[...].reshape(256, 256), cg)
    for l in range(4):
        lanes = slice(256 * l, 256 * l + 256)
        h, _ = gelu_both(mm(n1, we_ref[:, lanes]))
        hh_ref[:, lanes] = h.astype(BF16)
    h_ref[0] = hh_ref[0:64]
    h_ref[33] = hh_ref[64:128]

    rows32 = lax.broadcasted_iota(jnp.int32, (32, 1024), 0)

    def side(place, mid, above, below, taps):
        up = jnp.where(rows32 == 0, above, pltpu.roll(mid, 1, 0))
        down = jnp.where(rows32 == 31, below, pltpu.roll(mid, 31, 0))
        whole = (
            kf_ref[taps[0] : taps[0] + 1] * up
            + kf_ref[taps[1] : taps[1] + 1] * mid
            + kf_ref[taps[2] : taps[2] + 1] * down
        )
        for i in range(32):
            side_ref[place, i] = whole[i : i + 1]

    side(
        0,
        hh_ref[128:160].astype(F32),
        hh_ref[192:208].astype(F32)[15:16],
        hh_ref[224:240].astype(F32)[15:16],
        (0, 3, 6),
    )
    side(
        1,
        hh_ref[160:192].astype(F32),
        hh_ref[208:224].astype(F32)[0:1],
        hh_ref[240:256].astype(F32)[0:1],
        (2, 5, 8),
    )

    io64 = lax.broadcasted_iota(jnp.int32, (64, 128), 0)

    def depthwise(r, lanes, taps):
        a0 = h_ref[r, :, lanes].astype(F32)
        a1 = h_ref[r + 1, :, lanes].astype(F32)
        a2 = h_ref[r + 2, :, lanes].astype(F32)

        def three(j):
            return (
                kf_ref[taps[j] : taps[j] + 1, lanes] * a0
                + kf_ref[taps[3 + j] : taps[3 + j] + 1, lanes] * a1
                + kf_ref[taps[6 + j] : taps[6 + j] + 1, lanes] * a2
            )

        left = jnp.where(io64 == 0, side_ref[0, r, :, lanes], pltpu.roll(three(0), 1, 0))
        right = jnp.where(io64 == 63, side_ref[1, r, :, lanes], pltpu.roll(three(2), 63, 0))
        return three(1) + left + right

    forward_taps = tuple(range(9))
    backward_taps = tuple(range(8, -1, -1))

    def a2a_start(src, dst, k, q):
        pltpu.make_async_copy(src.at[64 * k + me], dst.at[64 * k + me], rsem.at[q, k]).start()

        def step(t, carry):
            qx = lax.rem(px + lax.rem(t, 4), 4)
            qy = lax.rem(py + lax.rem(lax.div(t, 4), 4), 4)
            qz = lax.rem(pz + lax.div(t, 16), 4)
            pg = lax.div(qx, 2) * 4 + qy
            pe = qz * 2 + lax.rem(qx, 2)
            pltpu.make_async_remote_copy(
                src_ref=src.at[64 * k + pg * 8 + pe],
                dst_ref=dst.at[64 * k + me],
                send_sem=ssem.at[q, k],
                recv_sem=rsem.at[q, k],
                device_id=(2 * pg + core, pe),
                device_id_type=MESH,
            ).start()
            return carry

        lax.fori_loop(1, 64, step, 0)

    def a2a_wait(dst, k, q):
        whole = dst.at[pl.ds(64 * k, 64)]
        pltpu.make_async_copy(whole, whole, rsem.at[q, k]).wait()

    def a2a_wait_send(src, k, q):
        part = src.at[pl.ds(64 * k, 63)]
        pltpu.make_async_copy(part, part, ssem.at[q, k]).wait()

    def shrink_block(b, carry):
        def one_row(rr, inner):
            r = 4 * b + rr
            for l in range(8):
                lanes = slice(128 * l, 128 * l + 128)
                h2, slope = gelu_both(depthwise(r, lanes, forward_taps))
                blk_ref[rr, :, lanes] = h2.astype(BF16)
                s2_ref[r, :, lanes] = slope.astype(BF16)
            return inner

        lax.fori_loop(0, 4, one_row, 0)
        here = pl.ds(16 * b, 16)
        added = mm(blk_ref[...].reshape(256, 1024), ws_ref[...])
        x1 = (x_ref[here].reshape(256, 256).astype(F32) + added).astype(BF16)
        x1_ref[here] = x1.reshape(16, 16, 256)
        n2h_ref[here] = norm(x1, gg).reshape(16, 16, 256)
        return carry

    for k in range(2):
        lax.fori_loop(4 * k, 4 * k + 4, shrink_block, 0)
        a2a_start(n2h_ref, rb_ref, k, 0)

    perm = perm_ref
    lane_head = lax.broadcasted_iota(jnp.int32, (64, 256), 1) // 32
    masks = [(lane_head == h).astype(F32) for h in range(HEADS)]
    masks_low = [m.astype(BF16) for m in masks]

    def spread(values):
        return jnp.concatenate([values * masks_low[h] for h in range(HEADS)], axis=0)

    def fold(product):
        total = product[0:64] * masks[0]
        for h in range(1, HEADS):
            total = total + product[64 * h : 64 * h + 64] * masks[h]
        return total

    def to_sets(src, dst, k):
        for i in range(4):
            block = src[64 * k + 16 * i : 64 * k + 16 * i + 16].reshape(256, 256)
            dst[16 * k : 16 * k + 16, 16 * i : 16 * i + 16, :] = (
                mm(perm[...], block).astype(BF16).reshape(16, 16, 256)
            )

    def from_sets(src, dst, k):
        for i in range(4):
            block = src[16 * k : 16 * k + 16, 16 * i : 16 * i + 16, :].reshape(256, 256)
            dst[64 * k + 16 * i : 64 * k + 16 * i + 16] = (
                mm(perm[...], block).astype(BF16).reshape(16, 16, 256)
            )

    scale = 1.0 / math.sqrt(32.0)

    def attend_set(s, carry):
        q_blk = spread(qs_ref[s])
        scores = mm_nt(ks_ref[s], q_blk) * scale + bias_ref[...]
        top = jnp.max(scores, axis=0, keepdims=True)
        e = jnp.exp(scores - top)
        probs = e * (1.0 / jnp.sum(e, axis=0, keepdims=True))
        ps_ref[s] = probs
        mxs_ref[s] = fold(mm_tn(probs.astype(BF16), vs_ref[s])).astype(BF16)
        return carry

    for k in range(2):
        a2a_wait(rb_ref, k, 0)
        to_sets(rb_ref, n2s_ref, k)

        def qkv_block(i, carry):
            here = pl.ds(16 * k + 4 * i, 4)
            n2 = n2s_ref[here].reshape(256, 256)
            qs_ref[here] = mm(n2, wqkv_ref[:, 0:256]).astype(BF16).reshape(4, 64, 256)
            ks_ref[here] = mm(n2, wqkv_ref[:, 256:512]).astype(BF16).reshape(4, 64, 256)
            vs_ref[here] = mm(n2, wqkv_ref[:, 512:768]).astype(BF16).reshape(4, 64, 256)
            return carry

        lax.fori_loop(0, 4, qkv_block, 0)
        lax.fori_loop(16 * k, 16 * k + 16, attend_set, 0)
        from_sets(mxs_ref, mx_ref, k)
        a2a_start(mx_ref, mh_ref, k, 1)

    def mlp_block(b, carry):
        here = pl.ds(16 * b, 16)
        attended = mm(mh_ref[here].reshape(256, 256), wmix_ref[...]).astype(BF16)
        x2 = (x1_ref[here].reshape(256, 256).astype(F32) + attended.astype(F32)).astype(BF16)
        x2_ref[here] = x2.reshape(16, 16, 256)
        n3 = norm(x2, mg)
        cot = cot_ref[here].reshape(256, 256)
        back = jnp.zeros((256, 256), F32)
        for l in range(4):
            lanes = slice(256 * l, 256 * l + 256)
            h3, slope = gelu_both(mm(n3, ww_ref[:, lanes]))
            h3_ref[pl.ds(4 * b, 4), :, lanes] = h3.astype(BF16).reshape(4, 64, 256)
            du3 = (mm_nt(cot, wn_ref[lanes, :]) * slope).astype(BF16)
            back = back + mm_nt(du3, ww_ref[:, lanes])
        dx2 = (cot.astype(F32) + norm_back(back, x2, mg)).astype(BF16)
        dx2_ref[here] = dx2.reshape(16, 16, 256)
        dm_ref[here] = mm_nt(dx2, wmix_ref[...]).astype(BF16).reshape(16, 16, 256)
        return carry

    for k in range(2):
        a2a_wait(mh_ref, k, 1)
        lax.fori_loop(4 * k, 4 * k + 4, mlp_block, 0)
        a2a_start(dm_ref, rb2_ref, k, 2)

    def out_block(b, carry):
        here = pl.ds(16 * b, 16)
        h3 = h3_ref[pl.ds(4 * b, 4)].reshape(256, 1024)
        out = x2_ref[here].reshape(256, 256).astype(F32) + mm(h3, wn_ref[...])
        out_ref[here] = out.astype(BF16).reshape(16, 16, 256)
        return carry

    lax.fori_loop(0, 8, out_block, 0)
    g_ref[:, 768:1024] = mm_tn(
        mh_ref[...].reshape(2048, 256), dx2_ref[...].reshape(2048, 256)
    )

    def attend_back_set(s, carry):
        q_blk = spread(qs_ref[s])
        d_blk = spread(dns_ref[s])
        probs = ps_ref[s]
        dprobs = mm_nt(vs_ref[s], d_blk)
        centre = jnp.sum(probs * dprobs, axis=0, keepdims=True)
        dscores = (probs * (dprobs - centre) * scale).astype(BF16)
        dv_ref[s] = mm(probs.astype(BF16), d_blk).astype(BF16)
        dk_ref[s] = mm(dscores, q_blk).astype(BF16)
        dq_ref[s] = fold(mm_tn(dscores, ks_ref[s])).astype(BF16)
        return carry

    for k in range(2):
        a2a_wait(rb2_ref, k, 2)
        to_sets(rb2_ref, dns_ref, k)
        lax.fori_loop(16 * k, 16 * k + 16, attend_back_set, 0)

        def dn_block(i, carry):
            here = pl.ds(16 * k + 4 * i, 4)
            total = (
                mm_nt(dq_ref[here].reshape(256, 256), wqkv_ref[:, 0:256])
                + mm_nt(dk_ref[here].reshape(256, 256), wqkv_ref[:, 256:512])
                + mm_nt(dv_ref[here].reshape(256, 256), wqkv_ref[:, 512:768])
            )
            mxs_ref[here] = total.astype(BF16).reshape(4, 64, 256)
            return carry

        lax.fori_loop(0, 4, dn_block, 0)
        from_sets(mxs_ref, dn_ref, k)
        a2a_start(dn_ref, dnh_ref, k, 3)

    n2t = n2s_ref[...].reshape(2048, 256)
    g_ref[:, 0:256] = mm_tn(n2t, dq_ref[...].reshape(2048, 256))
    g_ref[:, 256:512] = mm_tn(n2t, dk_ref[...].reshape(2048, 256))
    g_ref[:, 512:768] = mm_tn(n2t, dv_ref[...].reshape(2048, 256))
    for cb in range(8):
        gb_ref[cb] = g_ref[:, 128 * cb : 128 * cb + 128].astype(BF16).reshape(16, 16, 128)

    def along(axis, count, source, target, q):
        mine = col if axis == 1 else row

        def step(t, carry):
            peer = lax.rem(mine + t, count)
            dev = (row, peer) if axis == 1 else (peer, col)
            pltpu.make_async_remote_copy(
                src_ref=source(peer), dst_ref=target(mine), send_sem=as_sem.at[q],
                recv_sem=ar_sem.at[q], device_id=dev, device_id_type=MESH,
            ).start()
            return carry

        lax.fori_loop(1, count, step, 0)

    def wait_part(ref, sem):
        pltpu.make_async_copy(ref, ref, sem).wait()

    along(1, ncol, lambda p: gb_ref.at[p], lambda m: r1_ref.at[m], 0)
    r1_ref[col] = gb_ref[col]

    def cell_block(b, carry):
        here = pl.ds(16 * b, 16)
        dn = dnh_ref[here].reshape(256, 256).astype(F32)
        x1 = x1_ref[here].reshape(256, 256)
        dx1 = dx2_ref[here].reshape(256, 256).astype(F32) + norm_back(dn, x1, gg)
        dx1 = dx1.astype(BF16)
        dx1_ref[here] = dx1.reshape(16, 16, 256)
        for l in range(4):
            lanes = slice(256 * l, 256 * l + 256)
            slope = s2_ref[pl.ds(4 * b, 4), :, lanes].reshape(256, 256).astype(F32)
            du2 = mm_nt(dx1, ws_ref[lanes, :]) * slope
            h_ref[pl.ds(1 + 4 * b, 4), :, lanes] = du2.astype(BF16).reshape(4, 64, 256)
            for rr in range(4):
                edge_ref[0, 4 * b + rr, :, lanes] = du2[64 * rr : 64 * rr + 1]
                edge_ref[1, 4 * b + rr, :, lanes] = du2[64 * rr + 63 : 64 * rr + 64]
        return carry

    a2a_wait(dnh_ref, 0, 3)
    lax.fori_loop(0, 4, cell_block, 0)
    wait_part(r1_ref.at[pl.ds(0, 7)], ar_sem.at[0])
    total = r1_ref[0].astype(F32)
    for c in range(1, 8):
        total = total + r1_ref[c].astype(F32)
    t1_ref[...] = total.astype(BF16)
    along(0, nrow, lambda p: t1_ref.at[p], lambda m: r2_ref.at[m], 1)
    r2_ref[row] = t1_ref[row]
    a2a_wait(dnh_ref, 1, 3)
    lax.fori_loop(4, 8, cell_block, 0)
    for i in range(32):
        colf_ref[0, i : i + 1] = edge_ref[0, i]
        colf_ref[1, i : i + 1] = edge_ref[1, i]
    ccol_ref[0] = colf_ref[0].astype(BF16)
    ccol_ref[1] = colf_ref[1].astype(BF16)

    def d_source(idx):
        return (
            h_ref.at[1], h_ref.at[32], ccol_ref.at[0], ccol_ref.at[1],
            h_ref.at[1, pl.ds(0, 16)], h_ref.at[1, pl.ds(48, 16)],
            h_ref.at[32, pl.ds(0, 16)], h_ref.at[32, pl.ds(48, 16)],
        )[idx]

    def d_target(idx):
        return (
            drow_ref.at[1], drow_ref.at[0], dcol_ref.at[1], dcol_ref.at[0],
            dcorn_ref.at[3], dcorn_ref.at[2], dcorn_ref.at[1], dcorn_ref.at[0],
        )[idx]

    neighbours(edges, 0, d_source, d_target, ds_sem, dr_sem)

    wait_part(r2_ref.at[pl.ds(0, 15)], ar_sem.at[1])
    total = r2_ref[0].astype(F32)
    for r in range(1, 16):
        total = total + r2_ref[r].astype(F32)
    a3_ref[row] = (total * (1.0 / 512.0)).astype(BF16)
    along(0, nrow, lambda p: a3_ref.at[row], lambda m: a3_ref.at[m], 2)

    neighbours(edges, 1, d_source, d_target, ds_sem, dr_sem)
    h_ref[0] = drow_ref[0]
    h_ref[33] = drow_ref[1]
    side(
        0,
        dcol_ref[0].astype(F32),
        dcorn_ref[0].astype(F32)[15:16],
        dcorn_ref[2].astype(F32)[15:16],
        (8, 5, 2),
    )
    side(
        1,
        dcol_ref[1].astype(F32),
        dcorn_ref[1].astype(F32)[0:1],
        dcorn_ref[3].astype(F32)[0:1],
        (6, 3, 0),
    )

    def input_block(b, carry):
        def one_row(rr, inner):
            r = 4 * b + rr
            for l in range(8):
                lanes = slice(128 * l, 128 * l + 128)
                dh = depthwise(r, lanes, backward_taps)
                blk_ref[rr, :, lanes] = (dh * s1_ref[r, :, lanes].astype(F32)).astype(BF16)
            return inner

        lax.fori_loop(0, 4, one_row, 0)
        here = pl.ds(16 * b, 16)
        back = mm_nt(blk_ref[...].reshape(256, 1024), we_ref[...])
        x = x_ref[here].reshape(256, 256)
        out = dx1_ref[here].reshape(256, 256).astype(F32) + norm_back(back, x, cg)
        grad_ref[here] = out.astype(BF16).reshape(16, 16, 256)
        return carry

    lax.fori_loop(0, 3, input_block, 0)
    wait_part(a3_ref.at[pl.ds(0, 15)], ar_sem.at[2])
    a4_ref[col] = a3_ref[...]
    along(1, ncol, lambda p: a3_ref, lambda m: a4_ref.at[m], 3)
    lax.fori_loop(3, 8, input_block, 0)
    wait_part(a4_ref.at[pl.ds(0, 7)], ar_sem.at[3])
    for cb in range(6):
        qg_ref[:, 128 * cb : 128 * cb + 128] = a4_ref[cb].reshape(256, 128).astype(F32)
    for cb in range(2):
        mxg_ref[:, 128 * cb : 128 * cb + 128] = a4_ref[6 + cb].reshape(256, 128).astype(F32)

    neighbours(edges, 2, x_source, x_target, hs_sem, hr_sem)
    neighbours(edges, 2, d_source, d_target, ds_sem, dr_sem)
    for k in range(2):
        a2a_wait_send(n2h_ref, k, 0)
        a2a_wait_send(mx_ref, k, 1)
        a2a_wait_send(dm_ref, k, 2)
        a2a_wait_send(dn_ref, k, 3)
    wait_part(gb_ref.at[pl.ds(0, 7)], as_sem.at[0])
    wait_part(t1_ref.at[pl.ds(0, 15)], as_sem.at[1])
    wait_part(a3_ref.at[pl.ds(0, 15)], as_sem.at[2])
    wait_part(a4_ref.at[pl.ds(0, 7)], as_sem.at[3])


def body(
    block_input, cotangent, conv_gain, grid_gain, mlp_gain, expand_weight, depth_kernel,
    shrink_weight, qkv_weight, mix_weight, grid_bias, widen_weight, narrow_weight,
):
    taps = jnp.pad(depth_kernel.reshape(9, 1024).astype(F32), ((0, 7), (0, 0)))
    bias = grid_bias.transpose(2, 0, 1).reshape(64, 512)
    place = jnp.arange(256, dtype=jnp.int32)
    perm = (place[None, :] == ((place % 16) * 16 + place // 16)[:, None]).astype(BF16)
    cells = (128, 16, 256)
    sets = (32, 64, 256)
    vm = pltpu.VMEM
    dma = pltpu.SemaphoreType.DMA
    scratch = [
        vm((34, 64, 1024), BF16),
        vm((32, 64, 1024), BF16),
        vm((32, 64, 1024), BF16),
        vm((4, 64, 1024), BF16),
        vm((2, 32, 1, 1024), F32),
        vm((16, 16, 256), BF16),
        vm((256, 1024), BF16),
        vm((4, 32, 256), BF16),
        vm((2, 32, 1024), F32),
        vm((2, 32, 1, 1024), F32),
        vm(cells, BF16),
        vm(cells, BF16),
        vm(cells, BF16),
        vm(sets, BF16),
        vm(sets, BF16),
        vm(sets, BF16),
        vm(sets, BF16),
        vm((32, 64, 512), F32),
        vm(sets, BF16),
        vm(cells, BF16),
        vm(cells, BF16),
        vm(cells, BF16),
        vm((32, 64, 1024), BF16),
        vm(cells, BF16),
        vm(cells, BF16),
        vm(cells, BF16),
        vm(sets, BF16),
        vm(sets, BF16),
        vm(sets, BF16),
        vm(sets, BF16),
        vm(cells, BF16),
        vm(cells, BF16),
        vm(cells, BF16),
        vm((2, 64, 1024), BF16),
        vm((2, 32, 1024), BF16),
        vm((4, 16, 1024), BF16),
        vm((2, 32, 1024), BF16),
        vm((256, 1024), F32),
        vm((8, 16, 16, 128), BF16),
        vm((8, 16, 16, 128), BF16),
        vm((16, 16, 128), BF16),
        vm((16, 16, 128), BF16),
        vm((16, 16, 128), BF16),
        vm((8, 16, 16, 128), BF16),
        dma((4, 2)),
        dma((4, 2)),
        dma((8,)),
        dma((8,)),
        dma((8,)),
        dma((8,)),
        dma((4,)),
        dma((4,)),
    ]
    spec = pl.BlockSpec(memory_space=pltpu.VMEM)
    out, grad, qg, mxg = pl.pallas_call(
        kernel,
        out_shape=(
            jax.ShapeDtypeStruct(cells, BF16),
            jax.ShapeDtypeStruct(cells, BF16),
            jax.ShapeDtypeStruct((256, 768), F32),
            jax.ShapeDtypeStruct((256, 256), F32),
        ),
        in_specs=[spec] * 14,
        out_specs=(spec,) * 4,
        scratch_shapes=scratch,
        compiler_params=pltpu.CompilerParams(
            collective_id=0, has_side_effects=True, vmem_limit_bytes=60 * MIB
        ),
    )(
        block_input.reshape(cells), cotangent.reshape(cells), conv_gain[None], grid_gain[None],
        mlp_gain[None], expand_weight, taps, shrink_weight, qkv_weight, mix_weight, bias,
        widen_weight, narrow_weight, perm,
    )
    return out.reshape(32, 64, 256), grad.reshape(32, 64, 256), qg, mxg


def solution(mesh):
    whole = P()
    tile = P("row", "col", None)
    return jax.shard_map(
        body,
        mesh=mesh,
        in_specs=(tile, tile) + (whole,) * 11,
        out_specs=(tile, tile, whole, whole),
        check_vma=False,
    )
```

time: 467 us -> 152 us (0.33); the launches traced: 458 us -> 150 us
  waiting for transfers between devices: 172 us -> 0 us
  Pallas kernels: 0 us -> 140 us
  other arithmetic: 83.5 us -> 1.4 us
  matrix products: 71.2 us -> 0 us
  starting transfers between devices: 50.3 us -> 0 us
  local copies, waits for them, and re-layouts: 41.8 us -> 7.28 us
  blocking collectives: 23.8 us -> 0 us
  between operations: 15.2 us -> 0.67 us
    pallas_call x0 -> x1, Pallas kernels: none -> 140 us  [body(): pl.pallas_call(kernel, out_shape=(jax.ShapeDtypeStruct(cells, BF16), jax....]
    psum x1 -> x0, waiting for transfers between devices: 129 us -> none  [body(): qkv_total, mix_total = lax.psum((qkv_part, mix_part), ('row', 'col'))]
    dot_general x20 -> x0, matrix products: 71.2 us -> none  [the longest x6 19.5 us: dense_product(): return jnp.dot(left, right, preferred_element_type=jnp.float32)]
    convert_element_type x12 -> x1, other arithmetic: 41.5 us -> 0.76 us  [body(): (place[None, :] == (place % 16 * 16 + place // 16)[:, None]).astype(BF16)]
    all_to_all x3 -> x0, waiting for transfers between devices: 31.1 us -> none  [the longest x2 31.1 us: gather_sets(): lax.all_to_all(outgoing, ('row', 'col'), split_axis=0, concat_axis=0, til...]
    all_to_all x3 -> x0, starting transfers between devices: 27.5 us -> none  [the longest x2 20.9 us: gather_sets(): lax.all_to_all(outgoing, ('row', 'col'), split_axis=0, concat_axis=0, til...]
    all_to_all x1 -> x0, blocking collectives: 23.8 us -> none  [return_tiles(): lax.all_to_all(outgoing, ('row', 'col'), split_axis=0, concat_axis=0, til...]
    ppermute x8 -> x0, starting transfers between devices: 22.8 us -> none  [the longest x4 14 us: padded_2(): lax.ppermute(tail, axis, [(i, (i + 1) % count) for i in range(ends)])]
  transfers between devices with their start and end apart: 12 -> 0, of which waited for: 7 -> 0; matrix products, arithmetic and copies ran while one was open for 8% -> 0% of each run, Pallas kernels for 0% -> 0%
where the time goes in v1:
time: 152 us; the launch traced here: 150 us
  Pallas kernels  140 us (92%)
  local copies, waits for them, and re-layouts  7.28 us (5%)
    pallas_call x1, Pallas kernels, body(): pl.pallas_call(kernel, out_shape=(jax.ShapeDtypeStruct(cells, BF16), jax....  140 us
    unnamed x12, local copies, waits for them, and re-layouts  5.7 us

profile of v1, /device:TPU:3, one launch (start us, length us, event | category | flops | bytes accessed | tf_op | source)
XLA Modules:
  0.0 149.6 jit_solution(16447202448721655444)
XLA Ops:
  0.6 0.0 copy-start.2
  0.7 0.8 convert_element_type.9
  1.5 0.6 pad_convert_fusion.kf_ref
  2.1 0.8 fusion.perm_ref
  2.9 0.0 copy-done.2
  2.9 0.8 copy.18.bias_ref
  3.6 140.2 %shard_map.156 = (bf16[128,16,256]{2,1,0:T(8,128)(2,1)}, bf16[128,16,256]{2,1,0:T(8,128)(2,1)}, f32[256,768]{1,0:T(8,128)}, f32[256,256]{1,0:T(8,128)}) custom-call(bf16[128,16,256]{2,1,0:T(8,128)(2,1)} %bitcast.10, bf16[128,16,256]{2,1,0:T(8,128)(2,1)} %bitcast.11, f32[1,256]{1,0:T(1,128)} %bitcast.15, f32[1,256]{1,0:T(1,128)} %bitcast.16, ...), custom_call_target="tpu_custom_call" | custom-call | tf_op jit(solution)/shard_map/pallas_call | solution.py:603
  143.9 0.0 copy-start
  143.9 2.4 %copy.23 = bf16[32,64,256]{2,1,0:T(8,128)(2,1)} copy(bf16[32,64,256]{2,1,0:T(8,128)(2,1)} %bitcast.13) | data formatting | bytes 2097152
  146.3 0.0 copy-done
  146.3 0.0 copy-start.1
  146.3 1.0 copy.24
  147.2 0.5 copy-done.1
  147.8 0.0 copy-start.3
  147.8 0.9 copy.25
  148.7 0.2 copy-done.3
  148.9 0.7 copy.26
  (1 shorter events, 0.0 us)
Async XLA Ops:
  0.6 2.2 %copy-start.2 = (f32[8,64,64]{2,1,0:T(8,128)S(1)}, f32[8,64,64]{2,1,0:T(8,128)}, u32[]{:S(2)}) copy-start(f32[8,64,64]{2,1,0:T(8,128)} %param.23) | copy-start | bytes 393220
  143.9 2.4 %copy-start = (bf16[128,16,256]{2,1,0:T(8,128)(2,1)S(1)}, bf16[128,16,256]{2,1,0:T(8,128)(2,1)}, u32[]{:S(2)}) copy-start(bf16[128,16,256]{2,1,0:T(8,128)(2,1)} %get-tuple-element.9) | copy-start | bytes 3145732
  146.3 1.5 %copy-start.1 = (f32[256,768]{1,0:T(8,128)S(1)}, f32[256,768]{1,0:T(8,128)}, u32[]{:S(2)}) copy-start(f32[256,768]{1,0:T(8,128)} %get-tuple-element.18) | copy-start | bytes 2359300
  147.8 1.1 copy-start.3

commit v2 on v1

--- a/solution.py
+++ b/solution.py
@@ -16,6 +16,7 @@
 C0 = 0.7978845608028654
 C1 = 0.7978845608028654 * 0.044715
 MIB = 1024 * 1024
+GROUP = 4
 
 
 def mm(left, right):
@@ -52,7 +53,8 @@
     )
 
 
-def gelu_both(u):
+def gelu_both(wide):
+    u = wide.astype(BF16)
     w = C1 * (u * u)
     t = jnp.tanh(u * (w + C0))
     p = 0.5 * t + 0.5
@@ -63,7 +65,7 @@
 
 def kernel(
     x_ref, cot_ref, cg_ref, gg_ref, mg_ref, we_ref, kf_ref, ws_ref, wqkv_ref, wmix_ref, bias_ref,
-    ww_ref, wn_ref, perm_ref,
+    tap_ref, ww_ref, wn_ref, perm_ref,
     out_ref, grad_ref, qg_ref, mxg_ref,
     h_ref, s1_ref, s2_ref, blk_ref, side_ref, halo_ref, hh_ref, xcol_ref, colf_ref, edge_ref,
     x1_ref, n2h_ref, rb_ref, n2s_ref, qs_ref, ks_ref, vs_ref, ps_ref, mxs_ref, mx_ref, mh_ref,
@@ -112,8 +114,8 @@
         for l in range(4):
             lanes = slice(256 * l, 256 * l + 256)
             h, slope = gelu_both(mm(n1, we_ref[:, lanes]))
-            h_ref[pl.ds(1 + 4 * b, 4), :, lanes] = h.astype(BF16).reshape(4, 64, 256)
-            s1_ref[pl.ds(4 * b, 4), :, lanes] = slope.astype(BF16).reshape(4, 64, 256)
+            h_ref[pl.ds(1 + 4 * b, 4), :, lanes] = h.reshape(4, 64, 256)
+            s1_ref[pl.ds(4 * b, 4), :, lanes] = slope.reshape(4, 64, 256)
         return carry
 
     lax.fori_loop(0, 4, expand_block, 0)
@@ -163,7 +165,7 @@
     for l in range(4):
         lanes = slice(256 * l, 256 * l + 256)
         h, _ = gelu_both(mm(n1, we_ref[:, lanes]))
-        hh_ref[:, lanes] = h.astype(BF16)
+        hh_ref[:, lanes] = h
     h_ref[0] = hh_ref[0:64]
     h_ref[33] = hh_ref[64:128]
 
@@ -195,22 +197,27 @@
         (2, 5, 8),
     )
 
-    io64 = lax.broadcasted_iota(jnp.int32, (64, 128), 0)
+    io8 = lax.broadcasted_iota(jnp.int32, (8, 128), 0)
 
     def depthwise(r, lanes, taps):
-        a0 = h_ref[r, :, lanes].astype(F32)
-        a1 = h_ref[r + 1, :, lanes].astype(F32)
-        a2 = h_ref[r + 2, :, lanes].astype(F32)
+        a0 = h_ref[r, :, lanes].reshape(4, 16, 128)
+        a1 = h_ref[r + 1, :, lanes].reshape(4, 16, 128)
+        a2 = h_ref[r + 2, :, lanes].reshape(4, 16, 128)
 
         def three(j):
-            return (
-                kf_ref[taps[j] : taps[j] + 1, lanes] * a0
-                + kf_ref[taps[3 + j] : taps[3 + j] + 1, lanes] * a1
-                + kf_ref[taps[6 + j] : taps[6 + j] + 1, lanes] * a2
+            total = (
+                tap_ref[taps[j], :, lanes][None] * a0
+                + tap_ref[taps[3 + j], :, lanes][None] * a1
+                + tap_ref[taps[6 + j], :, lanes][None] * a2
             )
-
-        left = jnp.where(io64 == 0, side_ref[0, r, :, lanes], pltpu.roll(three(0), 1, 0))
-        right = jnp.where(io64 == 63, side_ref[1, r, :, lanes], pltpu.roll(three(2), 63, 0))
+            return total.reshape(64, 128).astype(F32)
+
+        left = pltpu.roll(three(0), 1, 0)
+        right = pltpu.roll(three(2), 63, 0)
+        first = jnp.where(io8 == 0, side_ref[0, r, :, lanes], left[0:8])
+        last = jnp.where(io8 == 7, side_ref[1, r, :, lanes], right[56:64])
+        left = jnp.concatenate([first, left[8:64]], axis=0)
+        right = jnp.concatenate([right[0:56], last], axis=0)
         return three(1) + left + right
 
     forward_taps = tuple(range(9))
@@ -251,8 +258,8 @@
             for l in range(8):
                 lanes = slice(128 * l, 128 * l + 128)
                 h2, slope = gelu_both(depthwise(r, lanes, forward_taps))
-                blk_ref[rr, :, lanes] = h2.astype(BF16)
-                s2_ref[r, :, lanes] = slope.astype(BF16)
+                blk_ref[rr, :, lanes] = h2
+                s2_ref[r, :, lanes] = slope
             return inner
 
         lax.fori_loop(0, 4, one_row, 0)
@@ -268,16 +275,17 @@
         a2a_start(n2h_ref, rb_ref, k, 0)
 
     perm = perm_ref
-    lane_head = lax.broadcasted_iota(jnp.int32, (64, 256), 1) // 32
-    masks = [(lane_head == h).astype(F32) for h in range(HEADS)]
+    lane_head = lax.broadcasted_iota(jnp.int32, (64, 128), 1) // 32
+    masks = [(lane_head == h).astype(F32) for h in range(4)]
     masks_low = [m.astype(BF16) for m in masks]
+    halves = ((slice(0, 128), slice(0, 256)), (slice(128, 256), slice(256, 512)))
 
     def spread(values):
-        return jnp.concatenate([values * masks_low[h] for h in range(HEADS)], axis=0)
+        return jnp.concatenate([values * masks_low[h] for h in range(4)], axis=0)
 
     def fold(product):
         total = product[0:64] * masks[0]
-        for h in range(1, HEADS):
+        for h in range(1, 4):
             total = total + product[64 * h : 64 * h + 64] * masks[h]
         return total
 
@@ -297,14 +305,19 @@
 
     scale = 1.0 / math.sqrt(32.0)
 
-    def attend_set(s, carry):
-        q_blk = spread(qs_ref[s])
-        scores = mm_nt(ks_ref[s], q_blk) * scale + bias_ref[...]
-        top = jnp.max(scores, axis=0, keepdims=True)
-        e = jnp.exp(scores - top)
-        probs = e * (1.0 / jnp.sum(e, axis=0, keepdims=True))
-        ps_ref[s] = probs
-        mxs_ref[s] = fold(mm_tn(probs.astype(BF16), vs_ref[s])).astype(BF16)
+    def attend_set(i, carry):
+        parts = [(GROUP * i + n, c, w) for n in range(GROUP) for c, w in halves]
+        scores = [mm_nt(ks_ref[s, :, c], spread(qs_ref[s, :, c])) for s, c, w in parts]
+        low = []
+        for (s, c, w), score in zip(parts, scores):
+            score = score * scale + bias_ref[:, w]
+            e = jnp.exp(score - jnp.max(score, axis=0, keepdims=True))
+            probs = e * (1.0 / jnp.sum(e, axis=0, keepdims=True))
+            ps_ref[s, :, w] = probs
+            low.append(probs.astype(BF16))
+        mixed = [mm_tn(p, vs_ref[s, :, c]) for (s, c, w), p in zip(parts, low)]
+        for (s, c, w), product in zip(parts, mixed):
+            mxs_ref[s, :, c] = fold(product).astype(BF16)
         return carry
 
     for k in range(2):
@@ -320,7 +333,7 @@
             return carry
 
         lax.fori_loop(0, 4, qkv_block, 0)
-        lax.fori_loop(16 * k, 16 * k + 16, attend_set, 0)
+        lax.fori_loop(16 // GROUP * k, 16 // GROUP * (k + 1), attend_set, 0)
         from_sets(mxs_ref, mx_ref, k)
         a2a_start(mx_ref, mh_ref, k, 1)
 
@@ -335,8 +348,8 @@
         for l in range(4):
             lanes = slice(256 * l, 256 * l + 256)
             h3, slope = gelu_both(mm(n3, ww_ref[:, lanes]))
-            h3_ref[pl.ds(4 * b, 4), :, lanes] = h3.astype(BF16).reshape(4, 64, 256)
-            du3 = (mm_nt(cot, wn_ref[lanes, :]) * slope).astype(BF16)
+            h3_ref[pl.ds(4 * b, 4), :, lanes] = h3.reshape(4, 64, 256)
+            du3 = mm_nt(cot, wn_ref[lanes, :]).astype(BF16) * slope
             back = back + mm_nt(du3, ww_ref[:, lanes])
         dx2 = (cot.astype(F32) + norm_back(back, x2, mg)).astype(BF16)
         dx2_ref[here] = dx2.reshape(16, 16, 256)
@@ -360,22 +373,28 @@
         mh_ref[...].reshape(2048, 256), dx2_ref[...].reshape(2048, 256)
     )
 
-    def attend_back_set(s, carry):
-        q_blk = spread(qs_ref[s])
-        d_blk = spread(dns_ref[s])
-        probs = ps_ref[s]
-        dprobs = mm_nt(vs_ref[s], d_blk)
-        centre = jnp.sum(probs * dprobs, axis=0, keepdims=True)
-        dscores = (probs * (dprobs - centre) * scale).astype(BF16)
-        dv_ref[s] = mm(probs.astype(BF16), d_blk).astype(BF16)
-        dk_ref[s] = mm(dscores, q_blk).astype(BF16)
-        dq_ref[s] = fold(mm_tn(dscores, ks_ref[s])).astype(BF16)
+    def attend_back_set(i, carry):
+        parts = [(GROUP * i + n, c, w) for n in range(GROUP) for c, w in halves]
+        d_blk = [spread(dns_ref[s, :, c]) for s, c, w in parts]
+        dprobs = [mm_nt(vs_ref[s, :, c], d) for (s, c, w), d in zip(parts, d_blk)]
+        dscores = []
+        for (s, c, w), dp, d in zip(parts, dprobs, d_blk):
+            probs = ps_ref[s, :, w]
+            weighted = probs * dp
+            centre = jnp.sum(weighted, axis=0, keepdims=True)
+            dscores.append(((weighted - probs * centre) * scale).astype(BF16))
+            dv_ref[s, :, c] = mm(probs.astype(BF16), d).astype(BF16)
+        for (s, c, w), ds in zip(parts, dscores):
+            dk_ref[s, :, c] = mm(ds, spread(qs_ref[s, :, c])).astype(BF16)
+        folded = [mm_tn(ds, ks_ref[s, :, c]) for (s, c, w), ds in zip(parts, dscores)]
+        for (s, c, w), product in zip(parts, folded):
+            dq_ref[s, :, c] = fold(product).astype(BF16)
         return carry
 
     for k in range(2):
         a2a_wait(rb2_ref, k, 2)
         to_sets(rb2_ref, dns_ref, k)
-        lax.fori_loop(16 * k, 16 * k + 16, attend_back_set, 0)
+        lax.fori_loop(16 // GROUP * k, 16 // GROUP * (k + 1), attend_back_set, 0)
 
         def dn_block(i, carry):
             here = pl.ds(16 * k + 4 * i, 4)
@@ -427,12 +446,14 @@
         dx1_ref[here] = dx1.reshape(16, 16, 256)
         for l in range(4):
             lanes = slice(256 * l, 256 * l + 256)
-            slope = s2_ref[pl.ds(4 * b, 4), :, lanes].reshape(256, 256).astype(F32)
-            du2 = mm_nt(dx1, ws_ref[lanes, :]) * slope
-            h_ref[pl.ds(1 + 4 * b, 4), :, lanes] = du2.astype(BF16).reshape(4, 64, 256)
+            slope = s2_ref[pl.ds(4 * b, 4), :, lanes].reshape(256, 256)
+            du2 = mm_nt(dx1, ws_ref[lanes, :]).astype(BF16) * slope
+            h_ref[pl.ds(1 + 4 * b, 4), :, lanes] = du2.reshape(4, 64, 256)
             for rr in range(4):
-                edge_ref[0, 4 * b + rr, :, lanes] = du2[64 * rr : 64 * rr + 1]
-                edge_ref[1, 4 * b + rr, :, lanes] = du2[64 * rr + 63 : 64 * rr + 64]
+                edge_ref[0, 4 * b + rr, :, lanes] = du2[64 * rr : 64 * rr + 16].astype(F32)[0:1]
+                edge_ref[1, 4 * b + rr, :, lanes] = (
+                    du2[64 * rr + 48 : 64 * rr + 64].astype(F32)[15:16]
+                )
         return carry
 
     a2a_wait(dnh_ref, 0, 3)
@@ -498,7 +519,7 @@
             for l in range(8):
                 lanes = slice(128 * l, 128 * l + 128)
                 dh = depthwise(r, lanes, backward_taps)
-                blk_ref[rr, :, lanes] = (dh * s1_ref[r, :, lanes].astype(F32)).astype(BF16)
+                blk_ref[rr, :, lanes] = dh.astype(BF16) * s1_ref[r, :, lanes]
             return inner
 
         lax.fori_loop(0, 4, one_row, 0)
@@ -538,6 +559,7 @@
     shrink_weight, qkv_weight, mix_weight, grid_bias, widen_weight, narrow_weight,
 ):
     taps = jnp.pad(depth_kernel.reshape(9, 1024).astype(F32), ((0, 7), (0, 0)))
+    wide_taps = jnp.broadcast_to(depth_kernel.reshape(9, 1, 1024), (9, 16, 1024))
     bias = grid_bias.transpose(2, 0, 1).reshape(64, 512)
     place = jnp.arange(256, dtype=jnp.int32)
     perm = (place[None, :] == ((place % 16) * 16 + place // 16)[:, None]).astype(BF16)
@@ -608,7 +630,7 @@
             jax.ShapeDtypeStruct((256, 768), F32),
             jax.ShapeDtypeStruct((256, 256), F32),
         ),
-        in_specs=[spec] * 14,
+        in_specs=[spec] * 15,
         out_specs=(spec,) * 4,
         scratch_shapes=scratch,
         compiler_params=pltpu.CompilerParams(
@@ -616,7 +638,7 @@
         ),
     )(
         block_input.reshape(cells), cotangent.reshape(cells), conv_gain[None], grid_gain[None],
-        mlp_gain[None], expand_weight, taps, shrink_weight, qkv_weight, mix_weight, bias,
+        mlp_gain[None], expand_weight, taps, shrink_weight, qkv_weight, mix_weight, bias, wide_taps,
         widen_weight, narrow_weight, perm,
     )
     return out.reshape(32, 64, 256), grad.reshape(32, 64, 256), qg, mxg

time: 152 us -> 128 us (0.84)
  Pallas kernels: 140 us -> 116 us
    pallas_call x1, Pallas kernels: 140 us -> 116 us  [body(): pl.pallas_call(kernel, out_shape=(jax.ShapeDtypeStruct(cells, BF16), jax....]
where the time goes in v2:
time: 128 us; the launch traced here: 126 us
  Pallas kernels  116 us (91%)
  local copies, waits for them, and re-layouts  8.03 us (6%)
  other arithmetic  1.4 us (1%)
    pallas_call x1, Pallas kernels, body(): pl.pallas_call(kernel, out_shape=(jax.ShapeDtypeStruct(cells, BF16), jax....  116 us
    unnamed x12, local copies, waits for them, and re-layouts  5.7 us

profile of v2, /device:TPU:3, one launch (start us, length us, event | category | flops | bytes accessed | tf_op | source)
XLA Modules:
  0.0 126.2 jit_solution(14837723769721913506)
XLA Ops:
  0.6 0.0 copy-start.2
  0.7 0.8 reshape.52
  1.5 0.6 pad_convert_fusion.kf_ref
  2.1 0.8 fusion.perm_ref
  2.9 0.0 copy-done.2
  2.9 0.8 copy.18.bias_ref
  3.6 0.7 broadcast_in_dim.19.tap_ref
  4.4 116.1 %shard_map.156 = (bf16[128,16,256]{2,1,0:T(8,128)(2,1)}, bf16[128,16,256]{2,1,0:T(8,128)(2,1)}, f32[256,768]{1,0:T(8,128)}, f32[256,256]{1,0:T(8,128)}) custom-call(bf16[128,16,256]{2,1,0:T(8,128)(2,1)} %bitcast.12, bf16[128,16,256]{2,1,0:T(8,128)(2,1)} %bitcast.13, f32[1,256]{1,0:T(1,128)} %bitcast.15, f32[1,256]{1,0:T(1,128)} %bitcast.16, ...), custom_call_target="tpu_custom_call" | custom-call | tf_op jit(solution)/shard_map/pallas_call | solution.py:625
  120.5 0.0 copy-start
  120.5 2.4 %copy.23 = bf16[32,64,256]{2,1,0:T(8,128)(2,1)} copy(bf16[32,64,256]{2,1,0:T(8,128)(2,1)} %bitcast.11) | data formatting | bytes 2097152
  122.9 0.0 copy-done
  122.9 0.0 copy-start.1
  122.9 1.0 copy.24
  123.8 0.5 copy-done.1
  124.4 0.0 copy-start.3
  124.4 0.9 copy.25
  125.3 0.2 copy-done.3
  125.5 0.7 copy.26
  (1 shorter events, 0.0 us)
Async XLA Ops:
  0.6 2.2 %copy-start.2 = (f32[8,64,64]{2,1,0:T(8,128)S(1)}, f32[8,64,64]{2,1,0:T(8,128)}, u32[]{:S(2)}) copy-start(f32[8,64,64]{2,1,0:T(8,128)} %param.23) | copy-start | bytes 393220
  120.5 2.4 %copy-start = (bf16[128,16,256]{2,1,0:T(8,128)(2,1)S(1)}, bf16[128,16,256]{2,1,0:T(8,128)(2,1)}, u32[]{:S(2)}) copy-start(bf16[128,16,256]{2,1,0:T(8,128)(2,1)} %get-tuple-element.9) | copy-start | bytes 3145732
  122.9 1.5 %copy-start.1 = (f32[256,768]{1,0:T(8,128)S(1)}, f32[256,768]{1,0:T(8,128)}, u32[]{:S(2)}) copy-start(f32[256,768]{1,0:T(8,128)} %get-tuple-element.18) | copy-start | bytes 2359300
  124.4 1.1 copy-start.3

commit v3 on v2

--- a/solution.py
+++ b/solution.py
@@ -64,13 +64,15 @@
 
 
 def kernel(
-    x_ref, cot_ref, cg_ref, gg_ref, mg_ref, we_ref, kf_ref, ws_ref, wqkv_ref, wmix_ref, bias_ref,
-    tap_ref, ww_ref, wn_ref, perm_ref,
-    out_ref, grad_ref, qg_ref, mxg_ref,
+    x_ref, cot_ref, cg_ref, gg_ref, mg_ref, we_ref, kd_ref, ws_ref, wqkv_ref, wmix_ref,
+    heads_ref, ww_ref, wn_ref,
+    out_hbm, grad_hbm, qg_hbm, mxg_hbm,
+    out_ref, grad_ref, qg_ref, mxg_ref, out_sem,
     h_ref, s1_ref, s2_ref, blk_ref, side_ref, halo_ref, hh_ref, xcol_ref, colf_ref, edge_ref,
     x1_ref, n2h_ref, rb_ref, n2s_ref, qs_ref, ks_ref, vs_ref, ps_ref, mxs_ref, mx_ref, mh_ref,
     x2_ref, h3_ref, dx2_ref, dm_ref, rb2_ref, dns_ref, dq_ref, dk_ref, dv_ref, dn_ref, dnh_ref, dx1_ref,
     drow_ref, dcol_ref, dcorn_ref, ccol_ref, g_ref, gb_ref, r1_ref, t1_ref, r2_ref, a3_ref, a4_ref,
+    kf_ref, perm, bias_ref,
     ssem, rsem, hs_sem, hr_sem, ds_sem, dr_sem, as_sem, ar_sem,
 ):
     row = lax.axis_index("row")
@@ -91,13 +93,24 @@
 
     barrier = pltpu.get_barrier_semaphore()
 
-    def greet(t, carry):
-        r = lax.rem(row + lax.div(t, ncol), nrow)
-        c = lax.rem(col + lax.rem(t, ncol), ncol)
+    def greet(r, c):
         pl.semaphore_signal(barrier, inc=1, device_id=(r, c), device_id_type=MESH)
-        return carry
-
-    lax.fori_loop(1, nrow * ncol, greet, 0)
+
+    def greet_core(t, carry):
+        greet(lax.rem(row + 2 * lax.div(t, 8), nrow), lax.rem(col + lax.rem(t, 8), ncol))
+        return carry
+
+    lax.fori_loop(1, 64, greet_core, 0)
+    for t in range(8):
+        greet(lax.rem(row + 1 + 2 * t, nrow), col)
+    for dr in (-1, 1):
+        for dc in (-1, 1):
+            there_r, there_c = row + dr, col + dc
+            ok = (there_r >= 0) & (there_r < nrow) & (there_c >= 0) & (there_c < ncol)
+            pl.when(ok)(functools.partial(greet, there_r, there_c))
+    rows_near = jnp.where((row == 0) | (row == nrow - 1), 1, 2)
+    cols_near = jnp.where((col == 0) | (col == ncol - 1), 1, 2)
+    greeted = 63 + 8 + rows_near * cols_near
 
     for i in range(32):
         colf_ref[0, i : i + 1, 0:256] = x_ref[4 * i].astype(F32)[0:1]
@@ -119,7 +132,7 @@
         return carry
 
     lax.fori_loop(0, 4, expand_block, 0)
-    pl.semaphore_wait(barrier, nrow * ncol - 1)
+    pl.semaphore_wait(barrier, greeted)
 
     def neighbours(edge, send, source, target, s_sem, r_sem):
         for idx, dr, dc in edge:
@@ -156,7 +169,28 @@
         )[idx]
 
     neighbours(edges, 0, x_source, x_target, hs_sem, hr_sem)
+
+    def narrow_block(b, carry):
+        cot = cot_ref[pl.ds(16 * b, 16)].reshape(256, 256)
+        for l in range(4):
+            lanes = slice(256 * l, 256 * l + 256)
+            back = mm_nt(cot, wn_ref[lanes, :]).astype(BF16)
+            h3_ref[pl.ds(4 * b, 4), :, lanes] = back.reshape(4, 64, 256)
+        return carry
+
     lax.fori_loop(4, 8, expand_block, 0)
+    for i in range(3):
+        taps = kd_ref[i].astype(F32)
+        for j in range(3):
+            tap = taps[j : j + 1]
+            kf_ref[3 * i + j : 3 * i + j + 1] = tap
+    at = lax.broadcasted_iota(jnp.int32, (256, 256), 0)
+    to = lax.broadcasted_iota(jnp.int32, (256, 256), 1)
+    perm[...] = jnp.where(to == (at % 16) * 16 + at // 16, 1.0, 0.0).astype(BF16)
+    for j in range(4):
+        pair = [heads_ref[2 * j + n].T for n in range(2)]
+        bias_ref[:, 128 * j : 128 * j + 128] = jnp.concatenate(pair, axis=1)
+    lax.fori_loop(0, 8, narrow_block, 0)
     neighbours(edges, 1, x_source, x_target, hs_sem, hr_sem)
 
     halo_ref[8:10] = xcol_ref[2].reshape(2, 16, 256)
@@ -171,16 +205,18 @@
 
     rows32 = lax.broadcasted_iota(jnp.int32, (32, 1024), 0)
 
-    def side(place, mid, above, below, taps):
-        up = jnp.where(rows32 == 0, above, pltpu.roll(mid, 1, 0))
-        down = jnp.where(rows32 == 31, below, pltpu.roll(mid, 31, 0))
+    def side(which, mid, above, below, taps, keep=(0, 32)):
+        size = mid.shape[0]
+        rows = rows32[0:size]
+        up = jnp.where(rows == 0, above, pltpu.roll(mid, 1, 0))
+        down = jnp.where(rows == size - 1, below, pltpu.roll(mid, size - 1, 0))
         whole = (
             kf_ref[taps[0] : taps[0] + 1] * up
             + kf_ref[taps[1] : taps[1] + 1] * mid
             + kf_ref[taps[2] : taps[2] + 1] * down
         )
-        for i in range(32):
-            side_ref[place, i] = whole[i : i + 1]
+        for i in range(*keep):
+            side_ref[which, i] = whole[i : i + 1]
 
     side(
         0,
@@ -200,17 +236,16 @@
     io8 = lax.broadcasted_iota(jnp.int32, (8, 128), 0)
 
     def depthwise(r, lanes, taps):
-        a0 = h_ref[r, :, lanes].reshape(4, 16, 128)
-        a1 = h_ref[r + 1, :, lanes].reshape(4, 16, 128)
-        a2 = h_ref[r + 2, :, lanes].reshape(4, 16, 128)
+        a0 = h_ref[r, :, lanes].astype(F32)
+        a1 = h_ref[r + 1, :, lanes].astype(F32)
+        a2 = h_ref[r + 2, :, lanes].astype(F32)
 
         def three(j):
-            total = (
-                tap_ref[taps[j], :, lanes][None] * a0
-                + tap_ref[taps[3 + j], :, lanes][None] * a1
-                + tap_ref[taps[6 + j], :, lanes][None] * a2
+            return (
+                kf_ref[taps[j] : taps[j] + 1, lanes] * a0
+                + kf_ref[taps[3 + j] : taps[3 + j] + 1, lanes] * a1
+                + kf_ref[taps[6 + j] : taps[6 + j] + 1, lanes] * a2
             )
-            return total.reshape(64, 128).astype(F32)
 
         left = pltpu.roll(three(0), 1, 0)
         right = pltpu.roll(three(2), 63, 0)
@@ -223,26 +258,49 @@
     forward_taps = tuple(range(9))
     backward_taps = tuple(range(8, -1, -1))
 
-    def a2a_start(src, dst, k, q):
-        pltpu.make_async_copy(src.at[64 * k + me], dst.at[64 * k + me], rsem.at[q, k]).start()
-
-        def step(t, carry):
-            qx = lax.rem(px + lax.rem(t, 4), 4)
-            qy = lax.rem(py + lax.rem(lax.div(t, 4), 4), 4)
-            qz = lax.rem(pz + lax.div(t, 16), 4)
-            pg = lax.div(qx, 2) * 4 + qy
-            pe = qz * 2 + lax.rem(qx, 2)
+    place = 16 * lax.rem(col, 4) + 2 * gi + lax.div(col, 4)
+    zh = lax.div(col, 4)
+    xh = lax.div(gi, 4)
+
+    def send_piece(src, dst, at, k, q, dev):
+        pltpu.make_async_remote_copy(
+            src_ref=src.at[at], dst_ref=dst.at[64 * k + me], send_sem=ssem.at[q, k],
+            recv_sem=rsem.at[q, k], device_id=dev, device_id_type=MESH,
+        ).start()
+
+    step2 = [(xh, zh), (1 - xh, 1 - zh)]
+    step4 = [(lax.rem(px + t, 4), lax.rem(py + t, 4), lax.rem(pz + t, 4)) for t in range(4)]
+    along_x = [(lax.div(s[0], 2), lax.rem(s[0], 2)) for s in step4]
+
+    def send_block(src, dst, b, q):
+        k, part = lax.div(b, 4), lax.rem(b, 4)
+        for t in range(1, 16):
+            og = step2[t % 2][0] * 4 + step4[t // 4][1]
+            oz = step2[(t // 2) % 2][1]
+            send_piece(src, dst, 16 * b + 2 * og + oz, k, q, (2 * og + core, 4 * oz + part))
+
+    def send_rest(src, dst, k, q):
+        for t in range(1, 4):
+            part = lax.rem(col + t, 4)
+            at = 64 * k + 16 * part + 2 * gi + zh
+            send_piece(src, dst, at, k, q, (row, 4 * zh + part))
+        pltpu.make_async_copy(src.at[64 * k + place], dst.at[64 * k + me], rsem.at[q, k]).start()
+
+    def send_home(src, dst, k, q):
+        pltpu.make_async_copy(src.at[64 * k + me], dst.at[64 * k + place], rsem.at[q, k]).start()
+
+        for t in range(1, 64):
+            (hi, lo), qy, qz = along_x[t % 4], step4[t // 4 % 4][1], step4[t // 16][2]
+            pg = hi * 4 + qy
+            pe = qz * 2 + lo
             pltpu.make_async_remote_copy(
                 src_ref=src.at[64 * k + pg * 8 + pe],
-                dst_ref=dst.at[64 * k + me],
+                dst_ref=dst.at[64 * k + place],
                 send_sem=ssem.at[q, k],
                 recv_sem=rsem.at[q, k],
                 device_id=(2 * pg + core, pe),
                 device_id_type=MESH,
             ).start()
-            return carry
-
-        lax.fori_loop(1, 64, step, 0)
 
     def a2a_wait(dst, k, q):
         whole = dst.at[pl.ds(64 * k, 64)]
@@ -252,7 +310,7 @@
         part = src.at[pl.ds(64 * k, 63)]
         pltpu.make_async_copy(part, part, ssem.at[q, k]).wait()
 
-    def shrink_block(b, carry):
+    def shrink_block(b, carry, before=True):
         def one_row(rr, inner):
             r = 4 * b + rr
             for l in range(8):
@@ -264,17 +322,20 @@
 
         lax.fori_loop(0, 4, one_row, 0)
         here = pl.ds(16 * b, 16)
+        if before:
+            send_block(n2h_ref, rb_ref, b - 1, 0)
         added = mm(blk_ref[...].reshape(256, 1024), ws_ref[...])
         x1 = (x_ref[here].reshape(256, 256).astype(F32) + added).astype(BF16)
         x1_ref[here] = x1.reshape(16, 16, 256)
         n2h_ref[here] = norm(x1, gg).reshape(16, 16, 256)
         return carry
 
-    for k in range(2):
-        lax.fori_loop(4 * k, 4 * k + 4, shrink_block, 0)
-        a2a_start(n2h_ref, rb_ref, k, 0)
-
-    perm = perm_ref
+    shrink_block(0, 0, before=False)
+    lax.fori_loop(1, 8, shrink_block, 0)
+    send_rest(n2h_ref, rb_ref, 0, 0)
+    send_block(n2h_ref, rb_ref, 7, 0)
+    send_rest(n2h_ref, rb_ref, 1, 0)
+
     lane_head = lax.broadcasted_iota(jnp.int32, (64, 128), 1) // 32
     masks = [(lane_head == h).astype(F32) for h in range(4)]
     masks_low = [m.astype(BF16) for m in masks]
@@ -335,10 +396,12 @@
         lax.fori_loop(0, 4, qkv_block, 0)
         lax.fori_loop(16 // GROUP * k, 16 // GROUP * (k + 1), attend_set, 0)
         from_sets(mxs_ref, mx_ref, k)
-        a2a_start(mx_ref, mh_ref, k, 1)
-
-    def mlp_block(b, carry):
+        send_home(mx_ref, mh_ref, k, 1)
+
+    def mlp_block(b, carry, before=True):
         here = pl.ds(16 * b, 16)
+        if before:
+            send_block(dm_ref, rb2_ref, b - 1, 2)
         attended = mm(mh_ref[here].reshape(256, 256), wmix_ref[...]).astype(BF16)
         x2 = (x1_ref[here].reshape(256, 256).astype(F32) + attended.astype(F32)).astype(BF16)
         x2_ref[here] = x2.reshape(16, 16, 256)
@@ -348,8 +411,9 @@
         for l in range(4):
             lanes = slice(256 * l, 256 * l + 256)
             h3, slope = gelu_both(mm(n3, ww_ref[:, lanes]))
-            h3_ref[pl.ds(4 * b, 4), :, lanes] = h3.reshape(4, 64, 256)
-            du3 = mm_nt(cot, wn_ref[lanes, :]).astype(BF16) * slope
+            rows = pl.ds(4 * b, 4)
+            du3 = h3_ref[rows, :, lanes].reshape(256, 256) * slope
+            h3_ref[rows, :, lanes] = h3.reshape(4, 64, 256)
             back = back + mm_nt(du3, ww_ref[:, lanes])
         dx2 = (cot.astype(F32) + norm_back(back, x2, mg)).astype(BF16)
         dx2_ref[here] = dx2.reshape(16, 16, 256)
@@ -358,8 +422,10 @@
 
     for k in range(2):
         a2a_wait(mh_ref, k, 1)
-        lax.fori_loop(4 * k, 4 * k + 4, mlp_block, 0)
-        a2a_start(dm_ref, rb2_ref, k, 2)
+        mlp_block(4 * k, 0, before=False)
+        lax.fori_loop(4 * k + 1, 4 * k + 4, mlp_block, 0)
+        send_block(dm_ref, rb2_ref, 4 * k + 3, 2)
+        send_rest(dm_ref, rb2_ref, k, 2)
 
     def out_block(b, carry):
         here = pl.ds(16 * b, 16)
@@ -369,6 +435,8 @@
         return carry
 
     lax.fori_loop(0, 8, out_block, 0)
+    store_out = pltpu.make_async_copy(out_ref, out_hbm, out_sem.at[8])
+    store_out.start()
     g_ref[:, 768:1024] = mm_tn(
         mh_ref[...].reshape(2048, 256), dx2_ref[...].reshape(2048, 256)
     )
@@ -408,7 +476,7 @@
 
         lax.fori_loop(0, 4, dn_block, 0)
         from_sets(mxs_ref, dn_ref, k)
-        a2a_start(dn_ref, dnh_ref, k, 3)
+        send_home(dn_ref, dnh_ref, k, 3)
 
     n2t = n2s_ref[...].reshape(2048, 256)
     g_ref[:, 0:256] = mm_tn(n2t, dq_ref[...].reshape(2048, 256))
@@ -456,8 +524,57 @@
                 )
         return carry
 
+    def store_grad(b):
+        here = pl.ds(16 * b, 16)
+        return pltpu.make_async_copy(grad_ref.at[here], grad_hbm.at[here], out_sem.at[b])
+
+    def input_block(b, carry):
+        def one_row(rr, inner):
+            r = 4 * b + rr
+            for l in range(8):
+                lanes = slice(128 * l, 128 * l + 128)
+                dh = depthwise(r, lanes, backward_taps)
+                blk_ref[rr, :, lanes] = dh.astype(BF16) * s1_ref[r, :, lanes]
+            return inner
+
+        lax.fori_loop(0, 4, one_row, 0)
+        here = pl.ds(16 * b, 16)
+        back = mm_nt(blk_ref[...].reshape(256, 1024), we_ref[...])
+        x = x_ref[here].reshape(256, 256)
+        out = dx1_ref[here].reshape(256, 256).astype(F32) + norm_back(back, x, cg)
+        grad_ref[here] = out.astype(BF16).reshape(16, 16, 256)
+        store_grad(b).start()
+        return carry
+
+    d_edges = edges + ((8, 0, -1), (9, 0, 1))
+
+    def d_source(idx):
+        return (
+            h_ref.at[1], h_ref.at[32], ccol_ref.at[0, pl.ds(16, 16)], ccol_ref.at[1, pl.ds(16, 16)],
+            h_ref.at[1, pl.ds(0, 16)], h_ref.at[1, pl.ds(48, 16)],
+            h_ref.at[32, pl.ds(0, 16)], h_ref.at[32, pl.ds(48, 16)],
+            ccol_ref.at[0, pl.ds(0, 16)], ccol_ref.at[1, pl.ds(0, 16)],
+        )[idx]
+
+    def d_target(idx):
+        return (
+            drow_ref.at[1], drow_ref.at[0],
+            dcol_ref.at[1, pl.ds(16, 16)], dcol_ref.at[0, pl.ds(16, 16)],
+            dcorn_ref.at[3], dcorn_ref.at[2], dcorn_ref.at[1], dcorn_ref.at[0],
+            dcol_ref.at[1, pl.ds(0, 16)], dcol_ref.at[0, pl.ds(0, 16)],
+        )[idx]
+
+    def columns(first):
+        for i in range(first, first + 16):
+            for n in range(2):
+                colf_ref[n, i : i + 1] = edge_ref[n, i]
+        for n in range(2):
+            ccol_ref[n, first : first + 16] = colf_ref[n, first : first + 16].astype(BF16)
+
     a2a_wait(dnh_ref, 0, 3)
     lax.fori_loop(0, 4, cell_block, 0)
+    columns(0)
+    neighbours(d_edges[8:], 0, d_source, d_target, ds_sem, dr_sem)
     wait_part(r1_ref.at[pl.ds(0, 7)], ar_sem.at[0])
     total = r1_ref[0].astype(F32)
     for c in range(1, 8):
@@ -467,35 +584,24 @@
     r2_ref[row] = t1_ref[row]
     a2a_wait(dnh_ref, 1, 3)
     lax.fori_loop(4, 8, cell_block, 0)
-    for i in range(32):
-        colf_ref[0, i : i + 1] = edge_ref[0, i]
-        colf_ref[1, i : i + 1] = edge_ref[1, i]
-    ccol_ref[0] = colf_ref[0].astype(BF16)
-    ccol_ref[1] = colf_ref[1].astype(BF16)
-
-    def d_source(idx):
-        return (
-            h_ref.at[1], h_ref.at[32], ccol_ref.at[0], ccol_ref.at[1],
-            h_ref.at[1, pl.ds(0, 16)], h_ref.at[1, pl.ds(48, 16)],
-            h_ref.at[32, pl.ds(0, 16)], h_ref.at[32, pl.ds(48, 16)],
-        )[idx]
-
-    def d_target(idx):
-        return (
-            drow_ref.at[1], drow_ref.at[0], dcol_ref.at[1], dcol_ref.at[0],
-            dcorn_ref.at[3], dcorn_ref.at[2], dcorn_ref.at[1], dcorn_ref.at[0],
-        )[idx]
-
-    neighbours(edges, 0, d_source, d_target, ds_sem, dr_sem)
-
+    columns(16)
+    neighbours(d_edges[:8], 0, d_source, d_target, ds_sem, dr_sem)
+    neighbours(d_edges[8:], 1, d_source, d_target, ds_sem, dr_sem)
+    for n, taps in ((0, (8, 5, 2)), (1, (6, 3, 0))):
+        early = dcol_ref[n, 0:16].astype(F32)
+        side(n, early, early[0:1], early[0:1], taps, (1, 15))
     wait_part(r2_ref.at[pl.ds(0, 15)], ar_sem.at[1])
     total = r2_ref[0].astype(F32)
     for r in range(1, 16):
         total = total + r2_ref[r].astype(F32)
     a3_ref[row] = (total * (1.0 / 512.0)).astype(BF16)
     along(0, nrow, lambda p: a3_ref.at[row], lambda m: a3_ref.at[m], 2)
-
-    neighbours(edges, 1, d_source, d_target, ds_sem, dr_sem)
+    lax.fori_loop(1, 3, input_block, 0)
+    wait_part(a3_ref.at[pl.ds(0, 15)], ar_sem.at[2])
+    a4_ref[col] = a3_ref[...]
+    along(1, ncol, lambda p: a3_ref, lambda m: a4_ref.at[m], 3)
+
+    neighbours(d_edges[:8], 1, d_source, d_target, ds_sem, dr_sem)
     h_ref[0] = drow_ref[0]
     h_ref[33] = drow_ref[1]
     side(
@@ -513,36 +619,24 @@
         (6, 3, 0),
     )
 
-    def input_block(b, carry):
-        def one_row(rr, inner):
-            r = 4 * b + rr
-            for l in range(8):
-                lanes = slice(128 * l, 128 * l + 128)
-                dh = depthwise(r, lanes, backward_taps)
-                blk_ref[rr, :, lanes] = dh.astype(BF16) * s1_ref[r, :, lanes]
-            return inner
-
-        lax.fori_loop(0, 4, one_row, 0)
-        here = pl.ds(16 * b, 16)
-        back = mm_nt(blk_ref[...].reshape(256, 1024), we_ref[...])
-        x = x_ref[here].reshape(256, 256)
-        out = dx1_ref[here].reshape(256, 256).astype(F32) + norm_back(back, x, cg)
-        grad_ref[here] = out.astype(BF16).reshape(16, 16, 256)
-        return carry
-
-    lax.fori_loop(0, 3, input_block, 0)
-    wait_part(a3_ref.at[pl.ds(0, 15)], ar_sem.at[2])
-    a4_ref[col] = a3_ref[...]
-    along(1, ncol, lambda p: a3_ref, lambda m: a4_ref.at[m], 3)
-    lax.fori_loop(3, 8, input_block, 0)
+    lax.fori_loop(0, 1, input_block, 0)
+    lax.fori_loop(3, 4, input_block, 0)
+    lax.fori_loop(4, 8, input_block, 0)
     wait_part(a4_ref.at[pl.ds(0, 7)], ar_sem.at[3])
     for cb in range(6):
         qg_ref[:, 128 * cb : 128 * cb + 128] = a4_ref[cb].reshape(256, 128).astype(F32)
     for cb in range(2):
         mxg_ref[:, 128 * cb : 128 * cb + 128] = a4_ref[6 + cb].reshape(256, 128).astype(F32)
 
+    stores = [
+        pltpu.make_async_copy(qg_ref, qg_hbm, out_sem.at[9]),
+        pltpu.make_async_copy(mxg_ref, mxg_hbm, out_sem.at[10]),
+    ]
+    for store in stores:
+        store.start()
+
     neighbours(edges, 2, x_source, x_target, hs_sem, hr_sem)
-    neighbours(edges, 2, d_source, d_target, ds_sem, dr_sem)
+    neighbours(d_edges, 2, d_source, d_target, ds_sem, dr_sem)
     for k in range(2):
         a2a_wait_send(n2h_ref, k, 0)
         a2a_wait_send(mx_ref, k, 1)
@@ -552,22 +646,47 @@
     wait_part(t1_ref.at[pl.ds(0, 15)], as_sem.at[1])
     wait_part(a3_ref.at[pl.ds(0, 15)], as_sem.at[2])
     wait_part(a4_ref.at[pl.ds(0, 7)], as_sem.at[3])
+    store_out.wait()
+    for b in range(8):
+        store_grad(b).wait()
+    for store in stores:
+        store.wait()
+
+
+def leave(a_in, b_in, c_in, d_in, a_out, b_out, c_out, d_out, a_mid, b_mid, c_mid, d_mid, sem):
+    loads, stores = [], []
+    for src, mid, dst, parts in (
+        (a_in, a_mid, a_out, 4), (b_in, b_mid, b_out, 4), (c_in, c_mid, c_out, 2), (d_in, d_mid, d_out, 1)
+    ):
+        size = src.shape[0] // parts
+        for n in range(parts):
+            here = pl.ds(n * size, size)
+            at = len(loads)
+            loads.append(pltpu.make_async_copy(src.at[here], mid.at[here], sem.at[0, at]))
+            stores.append(pltpu.make_async_copy(mid.at[here], dst.at[here], sem.at[1, at]))
+    for copy in loads:
+        copy.start()
+    for load, store in zip(loads, stores):
+        load.wait()
+        store.start()
+    for store in stores:
+        store.wait()
 
 
 def body(
     block_input, cotangent, conv_gain, grid_gain, mlp_gain, expand_weight, depth_kernel,
     shrink_weight, qkv_weight, mix_weight, grid_bias, widen_weight, narrow_weight,
 ):
-    taps = jnp.pad(depth_kernel.reshape(9, 1024).astype(F32), ((0, 7), (0, 0)))
-    wide_taps = jnp.broadcast_to(depth_kernel.reshape(9, 1, 1024), (9, 16, 1024))
-    bias = grid_bias.transpose(2, 0, 1).reshape(64, 512)
-    place = jnp.arange(256, dtype=jnp.int32)
-    perm = (place[None, :] == ((place % 16) * 16 + place // 16)[:, None]).astype(BF16)
     cells = (128, 16, 256)
     sets = (32, 64, 256)
     vm = pltpu.VMEM
     dma = pltpu.SemaphoreType.DMA
     scratch = [
+        vm(cells, BF16),
+        vm(cells, BF16),
+        vm((256, 768), F32),
+        vm((256, 256), F32),
+        dma((11,)),
         vm((34, 64, 1024), BF16),
         vm((32, 64, 1024), BF16),
         vm((32, 64, 1024), BF16),
@@ -612,35 +731,48 @@
         vm((16, 16, 128), BF16),
         vm((16, 16, 128), BF16),
         vm((8, 16, 16, 128), BF16),
+        vm((16, 1024), F32),
+        vm((256, 256), BF16),
+        vm((64, 512), F32),
         dma((4, 2)),
         dma((4, 2)),
         dma((8,)),
         dma((8,)),
-        dma((8,)),
-        dma((8,)),
+        dma((10,)),
+        dma((10,)),
         dma((4,)),
         dma((4,)),
     ]
     spec = pl.BlockSpec(memory_space=pltpu.VMEM)
+    anywhere = pl.BlockSpec(memory_space=pl.ANY)
+    shapes = (
+        jax.ShapeDtypeStruct(cells, BF16),
+        jax.ShapeDtypeStruct(cells, BF16),
+        jax.ShapeDtypeStruct((256, 768), F32),
+        jax.ShapeDtypeStruct((256, 256), F32),
+    )
     out, grad, qg, mxg = pl.pallas_call(
         kernel,
-        out_shape=(
-            jax.ShapeDtypeStruct(cells, BF16),
-            jax.ShapeDtypeStruct(cells, BF16),
-            jax.ShapeDtypeStruct((256, 768), F32),
-            jax.ShapeDtypeStruct((256, 256), F32),
-        ),
-        in_specs=[spec] * 15,
-        out_specs=(spec,) * 4,
+        out_shape=shapes,
+        in_specs=[spec] * 13,
+        out_specs=(anywhere,) * 4,
         scratch_shapes=scratch,
         compiler_params=pltpu.CompilerParams(
             collective_id=0, has_side_effects=True, vmem_limit_bytes=60 * MIB
         ),
     )(
         block_input.reshape(cells), cotangent.reshape(cells), conv_gain[None], grid_gain[None],
-        mlp_gain[None], expand_weight, taps, shrink_weight, qkv_weight, mix_weight, bias, wide_taps,
-        widen_weight, narrow_weight, perm,
-    )
+        mlp_gain[None], expand_weight, depth_kernel, shrink_weight, qkv_weight, mix_weight, grid_bias,
+        widen_weight, narrow_weight,
+    )
+    held = (out, grad, qg, mxg)
+    out, grad, qg, mxg = pl.pallas_call(
+        leave,
+        out_shape=shapes,
+        in_specs=[anywhere] * 4,
+        out_specs=(anywhere,) * 4,
+        scratch_shapes=[vm(a.shape, a.dtype) for a in shapes] + [dma((2, 12))],
+    )(*held)
     return out.reshape(32, 64, 256), grad.reshape(32, 64, 256), qg, mxg
 
 

time: 128 us -> 116 us (0.906); the launches traced: 126 us -> 116 us
  local copies, waits for them, and re-layouts: 8.03 us -> 0 us
  other arithmetic: 1.4 us -> 0 us
    unnamed x12 -> x0, local copies, waits for them, and re-layouts: 5.7 us -> none
    reshape x2 -> x0, local copies, waits for them, and re-layouts: 1.58 us -> none  [the longest x1 0.8 us: body(): taps = jnp.pad(depth_kernel.reshape(9, 1024).astype(F32), ((0, 7), (0, 0)))]
    pallas_call x1 -> x2, Pallas kernels: 116 us -> 115 us  [the longest x1 113 us: body(): pl.pallas_call(kernel, out_shape=shapes, in_specs=[spec] * 13, out_specs=...]
where the time goes in v3:
time: 116 us
  Pallas kernels  115 us (99%)
    pallas_call x1, Pallas kernels, body(): pl.pallas_call(kernel, out_shape=shapes, in_specs=[spec] * 13, out_specs=...  113 us
    pallas_call x1, Pallas kernels, body(): pl.pallas_call(leave, out_shape=shapes, in_specs=[anywhere] * 4, out_spec...  2.81 us

profile of v3, /device:TPU:3, one launch (start us, length us, event | category | flops | bytes accessed | tf_op | source)
XLA Modules:
  0.0 116.2 jit_solution(3906926058013289510)
XLA Ops:
  0.6 112.6 %shard_map.156 = (bf16[128,16,256]{2,1,0:T(8,128)(2,1)}, bf16[128,16,256]{2,1,0:T(8,128)(2,1)}, f32[256,768]{1,0:T(8,128)}, f32[256,256]{1,0:T(8,128)}) custom-call(bf16[128,16,256]{2,1,0:T(8,128)(2,1)} %bitcast.7, bf16[128,16,256]{2,1,0:T(8,128)(2,1)} %bitcast.8, f32[1,256]{1,0:T(1,128)} %bitcast.9, f32[1,256]{1,0:T(1,128)} %bitcast.10, f32[1,256]{1,0:T(1,128)} %bitcast.11, ...), custom_call_target="tpu_custom_call" | custom-call | tf_op jit(solution)/shard_map/pallas_call | solution.py:754
  113.3 2.8 %shard_map.157 = (bf16[128,16,256]{2,1,0:T(8,128)(2,1)}, bf16[128,16,256]{2,1,0:T(8,128)(2,1)}, f32[256,768]{1,0:T(8,128)}, f32[256,256]{1,0:T(8,128)}) custom-call(bf16[128,16,256]{2,1,0:T(8,128)(2,1)} %get-tuple-element.12.a_in, bf16[128,16,256]{2,1,0:T(8,128)(2,1)} %get-tuple-element.13.b_in, f32[256,768]{1,0:T(8,128)} %get-tuple-element.14.c_in, ...), custom_call_target="tpu_custom_call" | custom-call | tf_op jit(solution)/shard_map/pallas_call | solution.py:769

commit v4 on v3

--- a/solution.py
+++ b/solution.py
@@ -16,7 +16,7 @@
 C0 = 0.7978845608028654
 C1 = 0.7978845608028654 * 0.044715
 MIB = 1024 * 1024
-GROUP = 4
+GROUP = 8
 
 
 def mm(left, right):
@@ -123,15 +123,15 @@
     mg = mg_ref[...]
 
     def expand_block(b, carry):
-        n1 = norm(x_ref[pl.ds(16 * b, 16)].reshape(256, 256), cg)
+        n1 = norm(x_ref[pl.ds(64 * b, 64)].reshape(1024, 256), cg)
         for l in range(4):
             lanes = slice(256 * l, 256 * l + 256)
             h, slope = gelu_both(mm(n1, we_ref[:, lanes]))
-            h_ref[pl.ds(1 + 4 * b, 4), :, lanes] = h.reshape(4, 64, 256)
-            s1_ref[pl.ds(4 * b, 4), :, lanes] = slope.reshape(4, 64, 256)
-        return carry
-
-    lax.fori_loop(0, 4, expand_block, 0)
+            h_ref[pl.ds(1 + 16 * b, 16), :, lanes] = h.reshape(16, 64, 256)
+            s1_ref[pl.ds(16 * b, 16), :, lanes] = slope.reshape(16, 64, 256)
+        return carry
+
+    lax.fori_loop(0, 1, expand_block, 0)
     pl.semaphore_wait(barrier, greeted)
 
     def neighbours(edge, send, source, target, s_sem, r_sem):
@@ -171,14 +171,14 @@
     neighbours(edges, 0, x_source, x_target, hs_sem, hr_sem)
 
     def narrow_block(b, carry):
-        cot = cot_ref[pl.ds(16 * b, 16)].reshape(256, 256)
+        cot = cot_ref[pl.ds(64 * b, 64)].reshape(1024, 256)
         for l in range(4):
             lanes = slice(256 * l, 256 * l + 256)
             back = mm_nt(cot, wn_ref[lanes, :]).astype(BF16)
-            h3_ref[pl.ds(4 * b, 4), :, lanes] = back.reshape(4, 64, 256)
-        return carry
-
-    lax.fori_loop(4, 8, expand_block, 0)
+            h3_ref[pl.ds(16 * b, 16), :, lanes] = back.reshape(16, 64, 256)
+        return carry
+
+    lax.fori_loop(1, 2, expand_block, 0)
     for i in range(3):
         taps = kd_ref[i].astype(F32)
         for j in range(3):
@@ -190,7 +190,7 @@
     for j in range(4):
         pair = [heads_ref[2 * j + n].T for n in range(2)]
         bias_ref[:, 128 * j : 128 * j + 128] = jnp.concatenate(pair, axis=1)
-    lax.fori_loop(0, 8, narrow_block, 0)
+    lax.fori_loop(0, 2, narrow_block, 0)
     neighbours(edges, 1, x_source, x_target, hs_sem, hr_sem)
 
     halo_ref[8:10] = xcol_ref[2].reshape(2, 16, 256)
@@ -312,7 +312,7 @@
 
     def shrink_block(b, carry, before=True):
         def one_row(rr, inner):
-            r = 4 * b + rr
+            r = 8 * b + rr
             for l in range(8):
                 lanes = slice(128 * l, 128 * l + 128)
                 h2, slope = gelu_both(depthwise(r, lanes, forward_taps))
@@ -320,21 +320,23 @@
                 s2_ref[r, :, lanes] = slope
             return inner
 
-        lax.fori_loop(0, 4, one_row, 0)
-        here = pl.ds(16 * b, 16)
+        lax.fori_loop(0, 8, one_row, 0)
+        here = pl.ds(32 * b, 32)
         if before:
-            send_block(n2h_ref, rb_ref, b - 1, 0)
-        added = mm(blk_ref[...].reshape(256, 1024), ws_ref[...])
-        x1 = (x_ref[here].reshape(256, 256).astype(F32) + added).astype(BF16)
-        x1_ref[here] = x1.reshape(16, 16, 256)
-        n2h_ref[here] = norm(x1, gg).reshape(16, 16, 256)
-        return carry
-
-    shrink_block(0, 0, before=False)
-    lax.fori_loop(1, 8, shrink_block, 0)
-    send_rest(n2h_ref, rb_ref, 0, 0)
-    send_block(n2h_ref, rb_ref, 7, 0)
-    send_rest(n2h_ref, rb_ref, 1, 0)
+            send_block(n2h_ref, rb_ref, 2 * b - 2, 0)
+            send_block(n2h_ref, rb_ref, 2 * b - 1, 0)
+        added = mm(blk_ref[...].reshape(512, 1024), ws_ref[...])
+        x1 = (x_ref[here].reshape(512, 256).astype(F32) + added).astype(BF16)
+        x1_ref[here] = x1.reshape(32, 16, 256)
+        n2h_ref[here] = norm(x1, gg).reshape(32, 16, 256)
+        return carry
+
+    for k in range(2):
+        shrink_block(2 * k, 0, before=False)
+        shrink_block(2 * k + 1, 0)
+        send_block(n2h_ref, rb_ref, 4 * k + 2, 0)
+        send_block(n2h_ref, rb_ref, 4 * k + 3, 0)
+        send_rest(n2h_ref, rb_ref, k, 0)
 
     lane_head = lax.broadcasted_iota(jnp.int32, (64, 128), 1) // 32
     masks = [(lane_head == h).astype(F32) for h in range(4)]
@@ -386,55 +388,57 @@
         to_sets(rb_ref, n2s_ref, k)
 
         def qkv_block(i, carry):
-            here = pl.ds(16 * k + 4 * i, 4)
-            n2 = n2s_ref[here].reshape(256, 256)
-            qs_ref[here] = mm(n2, wqkv_ref[:, 0:256]).astype(BF16).reshape(4, 64, 256)
-            ks_ref[here] = mm(n2, wqkv_ref[:, 256:512]).astype(BF16).reshape(4, 64, 256)
-            vs_ref[here] = mm(n2, wqkv_ref[:, 512:768]).astype(BF16).reshape(4, 64, 256)
+            here = pl.ds(16 * k + 8 * i, 8)
+            n2 = n2s_ref[here].reshape(512, 256)
+            qs_ref[here] = mm(n2, wqkv_ref[:, 0:256]).astype(BF16).reshape(8, 64, 256)
+            ks_ref[here] = mm(n2, wqkv_ref[:, 256:512]).astype(BF16).reshape(8, 64, 256)
+            vs_ref[here] = mm(n2, wqkv_ref[:, 512:768]).astype(BF16).reshape(8, 64, 256)
             return carry
 
-        lax.fori_loop(0, 4, qkv_block, 0)
+        lax.fori_loop(0, 2, qkv_block, 0)
         lax.fori_loop(16 // GROUP * k, 16 // GROUP * (k + 1), attend_set, 0)
         from_sets(mxs_ref, mx_ref, k)
         send_home(mx_ref, mh_ref, k, 1)
 
     def mlp_block(b, carry, before=True):
-        here = pl.ds(16 * b, 16)
+        here = pl.ds(32 * b, 32)
         if before:
-            send_block(dm_ref, rb2_ref, b - 1, 2)
-        attended = mm(mh_ref[here].reshape(256, 256), wmix_ref[...]).astype(BF16)
-        x2 = (x1_ref[here].reshape(256, 256).astype(F32) + attended.astype(F32)).astype(BF16)
-        x2_ref[here] = x2.reshape(16, 16, 256)
+            send_block(dm_ref, rb2_ref, 2 * b - 2, 2)
+            send_block(dm_ref, rb2_ref, 2 * b - 1, 2)
+        attended = mm(mh_ref[here].reshape(512, 256), wmix_ref[...]).astype(BF16)
+        x2 = (x1_ref[here].reshape(512, 256).astype(F32) + attended.astype(F32)).astype(BF16)
+        x2_ref[here] = x2.reshape(32, 16, 256)
         n3 = norm(x2, mg)
-        cot = cot_ref[here].reshape(256, 256)
-        back = jnp.zeros((256, 256), F32)
+        cot = cot_ref[here].reshape(512, 256)
+        back = jnp.zeros((512, 256), F32)
         for l in range(4):
             lanes = slice(256 * l, 256 * l + 256)
             h3, slope = gelu_both(mm(n3, ww_ref[:, lanes]))
-            rows = pl.ds(4 * b, 4)
-            du3 = h3_ref[rows, :, lanes].reshape(256, 256) * slope
-            h3_ref[rows, :, lanes] = h3.reshape(4, 64, 256)
+            rows = pl.ds(8 * b, 8)
+            du3 = h3_ref[rows, :, lanes].reshape(512, 256) * slope
+            h3_ref[rows, :, lanes] = h3.reshape(8, 64, 256)
             back = back + mm_nt(du3, ww_ref[:, lanes])
         dx2 = (cot.astype(F32) + norm_back(back, x2, mg)).astype(BF16)
-        dx2_ref[here] = dx2.reshape(16, 16, 256)
-        dm_ref[here] = mm_nt(dx2, wmix_ref[...]).astype(BF16).reshape(16, 16, 256)
+        dx2_ref[here] = dx2.reshape(32, 16, 256)
+        dm_ref[here] = mm_nt(dx2, wmix_ref[...]).astype(BF16).reshape(32, 16, 256)
         return carry
 
     for k in range(2):
         a2a_wait(mh_ref, k, 1)
-        mlp_block(4 * k, 0, before=False)
-        lax.fori_loop(4 * k + 1, 4 * k + 4, mlp_block, 0)
+        mlp_block(2 * k, 0, before=False)
+        mlp_block(2 * k + 1, 0)
+        send_block(dm_ref, rb2_ref, 4 * k + 2, 2)
         send_block(dm_ref, rb2_ref, 4 * k + 3, 2)
         send_rest(dm_ref, rb2_ref, k, 2)
 
     def out_block(b, carry):
-        here = pl.ds(16 * b, 16)
-        h3 = h3_ref[pl.ds(4 * b, 4)].reshape(256, 1024)
-        out = x2_ref[here].reshape(256, 256).astype(F32) + mm(h3, wn_ref[...])
-        out_ref[here] = out.astype(BF16).reshape(16, 16, 256)
-        return carry
-
-    lax.fori_loop(0, 8, out_block, 0)
+        here = pl.ds(64 * b, 64)
+        h3 = h3_ref[pl.ds(16 * b, 16)].reshape(1024, 1024)
+        out = x2_ref[here].reshape(1024, 256).astype(F32) + mm(h3, wn_ref[...])
+        out_ref[here] = out.astype(BF16).reshape(64, 16, 256)
+        return carry
+
+    lax.fori_loop(0, 2, out_block, 0)
     store_out = pltpu.make_async_copy(out_ref, out_hbm, out_sem.at[8])
     store_out.start()
     g_ref[:, 768:1024] = mm_tn(
@@ -465,16 +469,16 @@
         lax.fori_loop(16 // GROUP * k, 16 // GROUP * (k + 1), attend_back_set, 0)
 
         def dn_block(i, carry):
-            here = pl.ds(16 * k + 4 * i, 4)
+            here = pl.ds(16 * k + 8 * i, 8)
             total = (
-                mm_nt(dq_ref[here].reshape(256, 256), wqkv_ref[:, 0:256])
-                + mm_nt(dk_ref[here].reshape(256, 256), wqkv_ref[:, 256:512])
-                + mm_nt(dv_ref[here].reshape(256, 256), wqkv_ref[:, 512:768])
+                mm_nt(dq_ref[here].reshape(512, 256), wqkv_ref[:, 0:256])
+                + mm_nt(dk_ref[here].reshape(512, 256), wqkv_ref[:, 256:512])
+                + mm_nt(dv_ref[here].reshape(512, 256), wqkv_ref[:, 512:768])
             )
-            mxs_ref[here] = total.astype(BF16).reshape(4, 64, 256)
+            mxs_ref[here] = total.astype(BF16).reshape(8, 64, 256)
             return carry
 
-        lax.fori_loop(0, 4, dn_block, 0)
+        lax.fori_loop(0, 2, dn_block, 0)
         from_sets(mxs_ref, dn_ref, k)
         send_home(dn_ref, dnh_ref, k, 3)
 
@@ -506,20 +510,20 @@
     r1_ref[col] = gb_ref[col]
 
     def cell_block(b, carry):
-        here = pl.ds(16 * b, 16)
-        dn = dnh_ref[here].reshape(256, 256).astype(F32)
-        x1 = x1_ref[here].reshape(256, 256)
-        dx1 = dx2_ref[here].reshape(256, 256).astype(F32) + norm_back(dn, x1, gg)
+        here = pl.ds(32 * b, 32)
+        dn = dnh_ref[here].reshape(512, 256).astype(F32)
+        x1 = x1_ref[here].reshape(512, 256)
+        dx1 = dx2_ref[here].reshape(512, 256).astype(F32) + norm_back(dn, x1, gg)
         dx1 = dx1.astype(BF16)
-        dx1_ref[here] = dx1.reshape(16, 16, 256)
+        dx1_ref[here] = dx1.reshape(32, 16, 256)
         for l in range(4):
             lanes = slice(256 * l, 256 * l + 256)
-            slope = s2_ref[pl.ds(4 * b, 4), :, lanes].reshape(256, 256)
+            slope = s2_ref[pl.ds(8 * b, 8), :, lanes].reshape(512, 256)
             du2 = mm_nt(dx1, ws_ref[lanes, :]).astype(BF16) * slope
-            h_ref[pl.ds(1 + 4 * b, 4), :, lanes] = du2.reshape(4, 64, 256)
-            for rr in range(4):
-                edge_ref[0, 4 * b + rr, :, lanes] = du2[64 * rr : 64 * rr + 16].astype(F32)[0:1]
-                edge_ref[1, 4 * b + rr, :, lanes] = (
+            h_ref[pl.ds(1 + 8 * b, 8), :, lanes] = du2.reshape(8, 64, 256)
+            for rr in range(8):
+                edge_ref[0, 8 * b + rr, :, lanes] = du2[64 * rr : 64 * rr + 16].astype(F32)[0:1]
+                edge_ref[1, 8 * b + rr, :, lanes] = (
                     du2[64 * rr + 48 : 64 * rr + 64].astype(F32)[15:16]
                 )
         return carry
@@ -528,23 +532,25 @@
         here = pl.ds(16 * b, 16)
         return pltpu.make_async_copy(grad_ref.at[here], grad_hbm.at[here], out_sem.at[b])
 
-    def input_block(b, carry):
+    def input_part(first, count):
+        cells, pieces = 256 * count, 16 * count
+
         def one_row(rr, inner):
-            r = 4 * b + rr
+            r = 4 * first + rr
             for l in range(8):
                 lanes = slice(128 * l, 128 * l + 128)
                 dh = depthwise(r, lanes, backward_taps)
                 blk_ref[rr, :, lanes] = dh.astype(BF16) * s1_ref[r, :, lanes]
             return inner
 
-        lax.fori_loop(0, 4, one_row, 0)
-        here = pl.ds(16 * b, 16)
-        back = mm_nt(blk_ref[...].reshape(256, 1024), we_ref[...])
-        x = x_ref[here].reshape(256, 256)
-        out = dx1_ref[here].reshape(256, 256).astype(F32) + norm_back(back, x, cg)
-        grad_ref[here] = out.astype(BF16).reshape(16, 16, 256)
-        store_grad(b).start()
-        return carry
+        lax.fori_loop(0, 4 * count, one_row, 0)
+        here = pl.ds(16 * first, pieces)
+        back = mm_nt(blk_ref[0 : 4 * count].reshape(cells, 1024), we_ref[...])
+        x = x_ref[here].reshape(cells, 256)
+        out = dx1_ref[here].reshape(cells, 256).astype(F32) + norm_back(back, x, cg)
+        grad_ref[here] = out.astype(BF16).reshape(pieces, 16, 256)
+        for b in range(first, first + count):
+            store_grad(b).start()
 
     d_edges = edges + ((8, 0, -1), (9, 0, 1))
 
@@ -572,7 +578,7 @@
             ccol_ref[n, first : first + 16] = colf_ref[n, first : first + 16].astype(BF16)
 
     a2a_wait(dnh_ref, 0, 3)
-    lax.fori_loop(0, 4, cell_block, 0)
+    lax.fori_loop(0, 2, cell_block, 0)
     columns(0)
     neighbours(d_edges[8:], 0, d_source, d_target, ds_sem, dr_sem)
     wait_part(r1_ref.at[pl.ds(0, 7)], ar_sem.at[0])
@@ -583,7 +589,7 @@
     along(0, nrow, lambda p: t1_ref.at[p], lambda m: r2_ref.at[m], 1)
     r2_ref[row] = t1_ref[row]
     a2a_wait(dnh_ref, 1, 3)
-    lax.fori_loop(4, 8, cell_block, 0)
+    lax.fori_loop(2, 4, cell_block, 0)
     columns(16)
     neighbours(d_edges[:8], 0, d_source, d_target, ds_sem, dr_sem)
     neighbours(d_edges[8:], 1, d_source, d_target, ds_sem, dr_sem)
@@ -596,7 +602,7 @@
         total = total + r2_ref[r].astype(F32)
     a3_ref[row] = (total * (1.0 / 512.0)).astype(BF16)
     along(0, nrow, lambda p: a3_ref.at[row], lambda m: a3_ref.at[m], 2)
-    lax.fori_loop(1, 3, input_block, 0)
+    input_part(1, 2)
     wait_part(a3_ref.at[pl.ds(0, 15)], ar_sem.at[2])
     a4_ref[col] = a3_ref[...]
     along(1, ncol, lambda p: a3_ref, lambda m: a4_ref.at[m], 3)
@@ -619,9 +625,10 @@
         (6, 3, 0),
     )
 
-    lax.fori_loop(0, 1, input_block, 0)
-    lax.fori_loop(3, 4, input_block, 0)
-    lax.fori_loop(4, 8, input_block, 0)
+    input_part(0, 1)
+    input_part(3, 2)
+    input_part(5, 2)
+    input_part(7, 1)
     wait_part(a4_ref.at[pl.ds(0, 7)], ar_sem.at[3])
     for cb in range(6):
         qg_ref[:, 128 * cb : 128 * cb + 128] = a4_ref[cb].reshape(256, 128).astype(F32)
@@ -690,7 +697,7 @@
         vm((34, 64, 1024), BF16),
         vm((32, 64, 1024), BF16),
         vm((32, 64, 1024), BF16),
-        vm((4, 64, 1024), BF16),
+        vm((8, 64, 1024), BF16),
         vm((2, 32, 1, 1024), F32),
         vm((16, 16, 256), BF16),
         vm((256, 1024), BF16),

time: 116 us -> 113 us (0.974); the launches traced: 116 us -> 112 us
  Pallas kernels: 115 us -> 111 us
    pallas_call x1, Pallas kernels: 113 us -> 108 us  [body(): pl.pallas_call(kernel, out_shape=shapes, in_specs=[spec] * 13, out_specs=...]
where the time goes in v4:
time: 113 us; the launch traced here: 112 us
  Pallas kernels  111 us (98%)
    pallas_call x1, Pallas kernels, body(): pl.pallas_call(kernel, out_shape=shapes, in_specs=[spec] * 13, out_specs=...  108 us
    pallas_call x1, Pallas kernels, body(): pl.pallas_call(leave, out_shape=shapes, in_specs=[anywhere] * 4, out_spec...  2.81 us

profile of v4, /device:TPU:3, one launch (start us, length us, event | category | flops | bytes accessed | tf_op | source)
XLA Modules:
  0.0 111.9 jit_solution(11393810107246859020)
XLA Ops:
  0.6 108.3 %shard_map.156 = (bf16[128,16,256]{2,1,0:T(8,128)(2,1)}, bf16[128,16,256]{2,1,0:T(8,128)(2,1)}, f32[256,768]{1,0:T(8,128)}, f32[256,256]{1,0:T(8,128)}) custom-call(bf16[128,16,256]{2,1,0:T(8,128)(2,1)} %bitcast.7, bf16[128,16,256]{2,1,0:T(8,128)(2,1)} %bitcast.8, f32[1,256]{1,0:T(1,128)} %bitcast.9, f32[1,256]{1,0:T(1,128)} %bitcast.10, f32[1,256]{1,0:T(1,128)} %bitcast.11, ...), custom_call_target="tpu_custom_call" | custom-call | tf_op jit(solution)/shard_map/pallas_call | solution.py:761
  108.9 2.8 %shard_map.157 = (bf16[128,16,256]{2,1,0:T(8,128)(2,1)}, bf16[128,16,256]{2,1,0:T(8,128)(2,1)}, f32[256,768]{1,0:T(8,128)}, f32[256,256]{1,0:T(8,128)}) custom-call(bf16[128,16,256]{2,1,0:T(8,128)(2,1)} %get-tuple-element.12.a_in, bf16[128,16,256]{2,1,0:T(8,128)(2,1)} %get-tuple-element.13.b_in, f32[256,768]{1,0:T(8,128)} %get-tuple-element.14.c_in, ...), custom_call_target="tpu_custom_call" | custom-call | tf_op jit(solution)/shard_map/pallas_call | solution.py:776
